TPU v7x, 32 devices: a whole 2x2x4 slice. The times are simulated.
32 devices in a mesh: batch: 2 (over core), grid: 16 (over z, y, x).
Axes of the slice: x: 2, y: 2, z: 4, core: 2. Of those that a mesh axis runs over, the one named last changes fastest.
Arguments:
- inputs: bfloat16 [16, 64, 64, 512], P('batch', 'grid'), may hold values from -17 to 17
- cotangent: bfloat16 [16, 64, 64, 512], P('batch', 'grid'), may hold values from -6 to 6
- dataset_ids: int32 [16], P('batch'), may hold values from 0 to 11
- channel_masks: int32 [12, 4], replicated, may hold values 0 or 1
- sample_counts: int32 [12], replicated, may hold values from 4 to 16
- norm1_gain: float32 [512], replicated, may hold values from 0.25 to 1.75
- norm1_bias: float32 [512], replicated, may hold values from -1 to 1
- spec_w1: bfloat16 [2, 8, 64, 64], replicated, may hold values from -0.5 to 0.5
- spec_b1: float32 [2, 512], replicated, may hold values from -1.5 to 1.5
- spec_w2: bfloat16 [2, 8, 64, 64], replicated, may hold values from -0.75 to 0.75
- spec_b2: float32 [2, 512], replicated, may hold values from -1.5 to 1.5
- norm2_gain: float32 [512], replicated, may hold values from 0.25 to 1.75
- norm2_bias: float32 [512], replicated, may hold values from -1 to 1
- mlp_in: bfloat16 [512, 2048], replicated, may hold values from -0.25 to 0.25
- mlp_in_bias: float32 [2048], replicated, may hold values from -1.5 to 1.5
- mlp_out: bfloat16 [2048, 512], replicated, may hold values from -0.25 to 0.25
- mlp_out_bias: float32 [512], replicated, may hold values from -1.5 to 1.5
Outputs:
- activations: bfloat16 [16, 64, 64, 512], P('batch', 'grid')
- input_grad: float32 [16, 64, 64, 512], P('batch', 'grid')
- norm1_gain_grad: float32 [512], replicated
- norm1_bias_grad: float32 [512], replicated
- spec_w1_grad: float32 [2, 8, 64, 64], replicated
- spec_b1_grad: float32 [2, 512], replicated
- spec_w2_grad: float32 [2, 8, 64, 64], replicated
- spec_b2_grad: float32 [2, 512], replicated
- norm2_gain_grad: float32 [512], replicated
- norm2_bias_grad: float32 [512], replicated
- mlp_in_grad: float32 [512, 2048], replicated
- mlp_in_bias_grad: float32 [2048], replicated
- mlp_out_grad: float32 [2048, 512], replicated
- mlp_out_bias_grad: float32 [512], replicated
All inputs are finite; a program needn't handle non-finite values.
Results may differ from a plain program's by a relative error of at most 0.017.
The roundings to bfloat16 on the way count: a program that leaves them out, or rounds other values in their place, can miss the bound.
Values may be sent and summed in bfloat16 or wider, within the bound.
A program may use at most 192 MiB of HBM per device.

v0:
```python
import math

import jax
import jax.numpy as jnp
from jax import lax
from jax.sharding import PartitionSpec as P

BLOCKS = 8
MODES = 32
BSIZE = 64


EPSILON = 1e-06
SHRINK = 0.1
PRECISE = lax.Precision.HIGHEST


def layer_norm(values, gain_vec, bias_vec):
    average = jnp.mean(values, axis=-1, keepdims=True)
    centred = values - average
    variance = jnp.mean(centred * centred, axis=-1, keepdims=True)
    return centred * lax.rsqrt(variance + EPSILON) * gain_vec + bias_vec


def gelu_exact(values):
    return jax.nn.gelu(values, approximate=False)


def smooth_shrink(values):
    return values - SHRINK * jnp.tanh(values / SHRINK)


def col_table(grid_cols, mode_count):
    col_idx = jnp.arange(grid_cols, dtype=jnp.int32)[:, None]
    mode_idx = jnp.arange(mode_count, dtype=jnp.int32)[None, :]
    angles = (col_idx * mode_idx % grid_cols).astype(jnp.float32) * (2.0 * math.pi / grid_cols)
    return jnp.stack([jnp.cos(angles), -jnp.sin(angles)], axis=1) * (1.0 / math.sqrt(grid_cols))


def inverse_col_table(col_tab):
    mode_count = col_tab.shape[2]
    doubling = jnp.where(jnp.arange(mode_count, dtype=jnp.int32) == 0, 1.0, 2.0).astype(jnp.float32)
    return jnp.transpose(col_tab, (2, 1, 0)) * doubling[:, None, None]


def row_table(height, mode_count):
    mode_idx = jnp.arange(mode_count, dtype=jnp.int32)
    frequency = jnp.where(mode_idx < mode_count // 2, mode_idx, height - mode_count + mode_idx)
    row_idx = jnp.arange(height, dtype=jnp.int32)
    angles = (frequency[:, None] * row_idx[None, :] % height).astype(jnp.float32) * (
        2.0 * math.pi / height
    )
    cosine = jnp.cos(angles)
    sine_vals = jnp.sin(angles)
    real_row = jnp.stack([cosine, sine_vals], axis=-1)
    imag_row = jnp.stack([-sine_vals, cosine], axis=-1)
    return jnp.stack([real_row, imag_row], axis=1) * (1.0 / math.sqrt(height))


def complex_block(weights):
    w_real = weights[0]
    w_imag = weights[1]
    top_rows = jnp.stack([w_real, w_imag], axis=2)
    bottom_rows = jnp.stack([-w_imag, w_real], axis=2)
    return jnp.stack([top_rows, bottom_rows], axis=1)


def complex_grad(grad_big):
    real_part = grad_big[:, 0, :, 0, :] + grad_big[:, 1, :, 1, :]
    imag_part = grad_big[:, 0, :, 1, :] - grad_big[:, 1, :, 0, :]
    return jnp.stack([real_part, imag_part], axis=0)


def mix_forward(values_bf, big_weight, bias_vec):
    product = jnp.einsum(
        "nrkb,krbsc->nskc", values_bf, big_weight, preferred_element_type=jnp.float32
    )
    return product + bias_vec.reshape(1, 2, BLOCKS, BSIZE)


def local(
    inputs,
    cotangent,
    dataset_ids,
    channel_masks,
    sample_counts,
    norm1_gain,
    norm1_bias,
    spec_w1,
    spec_b1,
    spec_w2,
    spec_b2,
    norm2_gain,
    norm2_bias,
    mlp_in,
    mlp_in_bias,
    mlp_out,
    mlp_out_bias,
):
    item_count, rows_here, grid_cols, feat_dim = inputs.shape
    height = rows_here * lax.axis_size("grid")
    col_tab = col_table(grid_cols, MODES)
    inv_tab = inverse_col_table(col_tab)
    row_tab = row_table(height, MODES)
    dataset_range = jnp.arange(channel_masks.shape[0], dtype=jnp.int32)
    onehot = (dataset_ids[:, None] == dataset_range[None, :]).astype(jnp.float32)
    group_live = jnp.dot(onehot, channel_masks.astype(jnp.float32), precision=PRECISE)
    chan_live = jnp.repeat(group_live, feat_dim // channel_masks.shape[1], axis=1)[:, None, None, :]
    item_weight = jnp.dot(onehot, sample_counts.astype(jnp.float32), precision=PRECISE) / 8.0
    w1_big = complex_block(spec_w1)
    w2_big = complex_block(spec_w2)
    inputs_f = inputs.astype(jnp.float32)
    normed_one, pull_norm1 = jax.vjp(layer_norm, inputs_f, norm1_gain, norm1_bias)
    col_spec = jnp.einsum("bhwd,wrq->bhqrd", normed_one, col_tab, precision=PRECISE)
    col_spec = col_spec.reshape(item_count, rows_here, MODES, 2 * feat_dim).astype(jnp.bfloat16)
    block_in = lax.all_to_all(col_spec, "grid", split_axis=2, concat_axis=1, tiled=True)
    count_here = block_in.shape[0]
    spread = block_in.reshape(count_here, height, -1, 2, feat_dim).astype(jnp.float32)
    mode_cols = spread.shape[2]
    mode_vals = jnp.einsum("bhqrd,pshr->bpqsd", spread, row_tab, precision=PRECISE).astype(
        jnp.bfloat16
    )
    mode_flat = mode_vals.reshape(-1, 2, BLOCKS, BSIZE)
    mixed_one = mix_forward(mode_flat, w1_big, spec_b1)
    act_one = gelu_exact(mixed_one).astype(jnp.bfloat16)
    mixed_two = mix_forward(act_one, w2_big, spec_b2)
    shrunk = smooth_shrink(mixed_two).astype(jnp.bfloat16)
    shrunk = shrunk.reshape(count_here, MODES, mode_cols, 2, feat_dim).astype(jnp.float32)
    row_back = jnp.einsum("bpqrd,prhs->bhqsd", shrunk, row_tab, precision=PRECISE)
    row_back = row_back.reshape(count_here, height, mode_cols, 2 * feat_dim).astype(jnp.bfloat16)
    returned_rows = lax.all_to_all(row_back, "grid", split_axis=1, concat_axis=2, tiled=True)
    kept_modes = mode_vals.reshape(count_here, MODES, mode_cols, 2 * feat_dim)
    back_spec = returned_rows.reshape(item_count, rows_here, MODES, 2, feat_dim).astype(jnp.float32)
    spatial = jnp.einsum("bhqrd,qrw->bhwd", back_spec, inv_tab, precision=PRECISE)
    residual = inputs_f + spatial * chan_live
    normed_two, pull_norm2 = jax.vjp(layer_norm, residual, norm2_gain, norm2_bias)
    normed_two_bf = normed_two.reshape(-1, feat_dim).astype(jnp.bfloat16)
    hidden = jnp.dot(normed_two_bf, mlp_in, preferred_element_type=jnp.float32) + mlp_in_bias
    act_two, pull_gelu = jax.vjp(gelu_exact, hidden)
    act_two_bf = act_two.astype(jnp.bfloat16)
    branch = jnp.dot(act_two_bf, mlp_out, preferred_element_type=jnp.float32) + mlp_out_bias
    activations = (residual + branch.reshape(residual.shape)).astype(jnp.bfloat16)
    grad_out = cotangent.astype(jnp.float32) * item_weight[:, None, None, None]
    grad_branch = grad_out.reshape(-1, feat_dim).astype(jnp.bfloat16)
    grad_mlp_out = jnp.einsum(
        "nf,nd->fd", act_two_bf, grad_branch, preferred_element_type=jnp.float32
    )
    grad_mlp_out_bias = jnp.sum(grad_branch.astype(jnp.float32), axis=0)
    grad_act_two = jnp.einsum("nd,fd->nf", grad_branch, mlp_out, preferred_element_type=jnp.float32)
    grad_hidden = pull_gelu(grad_act_two)[0].astype(jnp.bfloat16)
    grad_mlp_in = jnp.einsum(
        "nd,nf->df", normed_two_bf, grad_hidden, preferred_element_type=jnp.float32
    )
    grad_mlp_in_bias = jnp.sum(grad_hidden.astype(jnp.float32), axis=0)
    grad_normed_two = jnp.einsum(
        "nf,df->nd", grad_hidden, mlp_in, preferred_element_type=jnp.float32
    )
    grad_resid_norm, grad_gain_two, grad_bias_two = pull_norm2(
        grad_normed_two.reshape(residual.shape)
    )
    grad_resid = grad_out + grad_resid_norm
    mlp_grads = (
        grad_gain_two,
        grad_bias_two,
        grad_mlp_in,
        grad_mlp_in_bias,
        grad_mlp_out,
        grad_mlp_out_bias,
    )
    grad_spatial = grad_resid * chan_live
    grad_back = jnp.einsum("bhwd,qrw->bhqrd", grad_spatial, inv_tab, precision=PRECISE)
    grad_back = grad_back.reshape(item_count, rows_here, MODES, 2 * feat_dim).astype(jnp.bfloat16)
    grad_rows = lax.all_to_all(grad_back, "grid", split_axis=2, concat_axis=1, tiled=True)
    mode_cols = grad_rows.shape[2]
    grad_rows = grad_rows.reshape(item_count, height, mode_cols, 2, feat_dim).astype(jnp.float32)
    grad_shrunk = jnp.einsum("bhqrd,pshr->bpqsd", grad_rows, row_tab, precision=PRECISE)
    mode_flat = kept_modes.reshape(-1, 2, BLOCKS, BSIZE)
    mixed_one = mix_forward(mode_flat, w1_big, spec_b1)
    act_one, pull_act_one = jax.vjp(gelu_exact, mixed_one)
    act_one_bf = act_one.astype(jnp.bfloat16)
    mixed_two = mix_forward(act_one_bf, w2_big, spec_b2)
    shrunk_unused, pull_shrink = jax.vjp(smooth_shrink, mixed_two)
    grad_mixed_two = pull_shrink(grad_shrunk.reshape(mixed_two.shape))[0].astype(jnp.bfloat16)
    grad_w2_big = jnp.einsum(
        "nrkb,nskc->krbsc", act_one_bf, grad_mixed_two, preferred_element_type=jnp.float32
    )
    grad_spec_b2 = jnp.sum(grad_mixed_two.astype(jnp.float32), axis=0).reshape(2, feat_dim)
    grad_act_one = jnp.einsum(
        "nskc,krbsc->nrkb", grad_mixed_two, w2_big, preferred_element_type=jnp.float32
    )
    grad_mixed_one = pull_act_one(grad_act_one)[0].astype(jnp.bfloat16)
    grad_w1_big = jnp.einsum(
        "nrkb,nskc->krbsc", mode_flat, grad_mixed_one, preferred_element_type=jnp.float32
    )
    grad_spec_b1 = jnp.sum(grad_mixed_one.astype(jnp.float32), axis=0).reshape(2, feat_dim)
    grad_modes = jnp.einsum(
        "nskc,krbsc->nrkb", grad_mixed_one, w1_big, preferred_element_type=jnp.float32
    )
    grad_modes = grad_modes.reshape(item_count, MODES, mode_cols, 2, feat_dim)
    grad_col_spec = jnp.einsum("bpqrd,prhs->bhqsd", grad_modes, row_tab, precision=PRECISE)
    grad_col_spec = grad_col_spec.reshape(item_count, height, mode_cols, 2 * feat_dim).astype(
        jnp.bfloat16
    )
    grad_cols = lax.all_to_all(grad_col_spec, "grid", split_axis=1, concat_axis=2, tiled=True)
    grad_cols = grad_cols.reshape(item_count, rows_here, MODES, 2, feat_dim).astype(jnp.float32)
    grad_normed_one = jnp.einsum("bhqrd,wrq->bhwd", grad_cols, col_tab, precision=PRECISE)
    grad_input_norm, grad_gain_one, grad_bias_one = pull_norm1(grad_normed_one)
    input_grad = grad_resid + grad_input_norm
    mixer_grads = (
        grad_gain_one,
        grad_bias_one,
        complex_grad(grad_w1_big),
        grad_spec_b1,
        complex_grad(grad_w2_big),
        grad_spec_b2,
    )
    summed = tuple(lax.psum(mixer_grads + mlp_grads, ("batch", "grid")))
    return (activations, input_grad) + tuple(summed)


def solution(mesh):
    placed = (
        P("batch", "grid", None, None),
        P("batch", "grid", None, None),
        P("batch"),
        P(),
        P(),
        P(),
        P(),
        P(),
        P(),
        P(),
        P(),
        P(),
        P(),
        P(),
        P(),
        P(),
        P(),
    )
    return jax.shard_map(
        local,
        mesh=mesh,
        in_specs=placed,
        out_specs=(
            P("batch", "grid", None, None),
            P("batch", "grid", None, None),
            P(),
            P(),
            P(),
            P(),
            P(),
            P(),
            P(),
            P(),
            P(),
            P(),
            P(),
            P(),
        ),
        check_vma=False,
    )
```

profile of v0, /device:TPU:0, one launch (start us, length us, event | category | flops | bytes accessed | tf_op | source)
XLA Modules:
  0.0 664.3 jit_solution(4509580980097098783)
XLA Ops:
  12.6 4.5 convert_bitcast_fusion.1
  25.0 8.5 %all-to-all-start = ((bf16[8,4,32,1024]{3,1,0,2:T(4,128)(2,1)}), bf16[8,4,32,1024]{3,1,0,2:T(4,128)(2,1)}, u32[]{:S(2)}, u32[]{:S(2)}) async-start(bf16[8,4,32,1024]{3,1,0,2:T(4,128)(2,1)} %reshape.495), calls=%async_computation | async-start | bytes 4194304 | tf_op jit(solution)/shard_map/all_to_all | solution.py:116
  36.4 40.3 %all-to-all-done = bf16[8,4,32,1024]{3,1,0,2:T(4,128)(2,1)} async-done(((bf16[8,4,32,1024]{3,1,0,2:T(4,128)(2,1)}), bf16[8,4,32,1024]{3,1,0,2:T(4,128)(2,1)}, u32[]{:S(2)}, u32[]{:S(2)}) %all-to-all-start) | async-done | bytes 2097184 | tf_op jit(solution)/shard_map/all_to_all | solution.py:116
  84.8 4.8 fusion.73
  92.9 8.8 %multiply_convert_fusion.1 = (bf16[512,2,8,64]{0,3,1,2:T(8,128)(2,1)S(1)}, f32[512,2,8,64]{0,3,1,2:T(8,128)}, f32[8,2,64,512,1]{3,2,4,1,0:T(8,128)}) fusion(f32[2,8,64]{2,0,1:T(2,128)S(1)} %copy.139, bf16[512,2,8,64,1]{3,2,1,0,4:T(8,128)(2,1)} %bitcast.334, bf16[8,1,64,2,64]{2,4,1,3,0:T(8,128)(2,1)} %get-tuple-element.47, ...), kind=kOutput, calls=%fused_computation.96 | convolution fusion | flops 168951808 | bytes 6557696 | tf_op jit(solution)/shard_map/nrkb,krbsc->nskc/dot_general | solution.py:75
  116.8 7.0 %reshape.496 = bf16[8,64,2,1024]{3,2,0,1:T(2,128)(2,1)} reshape(bf16[8,64,2,2,512]{4,3,2,0,1:T(2,128)(2,1)} %copy.201) | data formatting | bytes 4194304 | tf_op jit(solution)/shard_map/convert_element_type | solution.py:130
  123.8 10.5 %all-to-all-start.1 = ((bf16[8,64,2,1024]{3,2,0,1:T(2,128)(2,1)}), bf16[8,64,2,1024]{3,2,0,1:T(2,128)(2,1)}, u32[]{:S(2)}, u32[]{:S(2)}) async-start(bf16[8,64,2,1024]{3,2,0,1:T(2,128)(2,1)} %reshape.496), calls=%async_computation.1 | async-start | bytes 4194304 | tf_op jit(solution)/shard_map/all_to_all | solution.py:131
  139.2 37.5 %all-to-all-done.1 = bf16[8,64,2,1024]{3,2,0,1:T(2,128)(2,1)} async-done(((bf16[8,64,2,1024]{3,2,0,1:T(2,128)(2,1)}), bf16[8,64,2,1024]{3,2,0,1:T(2,128)(2,1)}, u32[]{:S(2)}, u32[]{:S(2)}) %all-to-all-start.1) | async-done | bytes 2097184 | tf_op jit(solution)/shard_map/all_to_all | solution.py:131
  184.7 5.5 fusion.154
  193.6 41.5 %multiply_convert_fusion = (bf16[2048,2048]{1,0:T(8,128)(2,1)}, f32[2048,2048]{1,0:T(8,128)}, f32[2048,2048]{1,0:T(8,128)}) fusion(f32[2048]{0:T(1024)S(1)} %copy-done.61, bf16[2048,512]{1,0:T(8,128)(2,1)S(1)} %bitcast.343, bf16[512,2048]{1,0:T(8,128)(2,1)S(1)} %copy-done), kind=kOutput, calls=%fused_computation.4 | convolution fusion | flops 4571791360 | bytes 46145536 | tf_op jit(solution)/shard_map/dot_general | solution.py:138
  235.1 21.8 %convert_reduce_fusion = (f32[2048]{0:T(1024)S(1)}, bf16[2048,2048]{1,0:T(8,128)(2,1)}) fusion(f32[2048,2048]{1,0:T(8,128)} %get-tuple-element.35, bf16[2048,512]{1,0:T(8,128)(2,1)} %bitcast.341, bf16[2048,512]{1,0:T(8,128)(2,1)} %param.32, f32[2048,2048]{1,0:T(8,128)} %get-tuple-element.58, f32[2048]{0:T(1024)S(1)} %copy-done.61), kind=kOutput, calls=%fused_computation.2 | convolution fusion | flops 4366268416 | bytes 46153728 | tf_op jit(solution)/shard_map/nd,fd->nf/dot_general | solution.py:149
  257.0 7.1 %fusion.155 = (f32[512]{0:T(512)S(1)}, f32[2048,512]{1,0:T(8,128)S(1)}) fusion(bf16[2048,2048]{1,0:T(8,128)(2,1)} %get-tuple-element.66, bf16[512,2048]{1,0:T(8,128)(2,1)S(1)} %copy-done), kind=kOutput, calls=%fused_computation.239 | convolution fusion | flops 4296015360 | bytes 14682112 | tf_op jit(solution)/shard_map/nf,df->nd/dot_general | solution.py:155
  268.2 4.7 convolution_add_fusion
  279.1 7.4 %convert_bitcast_fusion = bf16[8,4,32,2,512]{4,2,1,0,3:T(8,128)(2,1)S(1)} fusion(f32[8,4,64,512]{3,2,1,0:T(8,128)} %get-tuple-element.38, bf16[8,4,64,512]{3,2,1,0:T(8,128)(2,1)} %param.18, f32[8,512]{1,0:T(8,128)S(1)} %copy-done.39, f32[8,4,64]{2,1,0:T(4,128)S(1)} %negate_multiply_fusion.3, f32[8]{0:T(128)S(1)} %copy-done.54, f32[32]{0:T(128)S(1)} %copy-done.56, ...), kind=kOutput, calls=%fused_computation.90 | convolution fusion | flops 811606016 | bytes 8429728 | tf_op jit(solution)/shard_map/bhwd,qrw->bhqrd/dot_general | solution.py:171
  294.3 10.2 %all-to-all-start.2 = ((bf16[8,4,32,1024]{3,1,0,2:T(4,128)(2,1)}), bf16[8,4,32,1024]{3,1,0,2:T(4,128)(2,1)}, u32[]{:S(2)}, u32[]{:S(2)}) async-start(bf16[8,4,32,1024]{3,1,0,2:T(4,128)(2,1)} %reshape.497), calls=%async_computation.2 | async-start | bytes 4194304 | tf_op jit(solution)/shard_map/all_to_all | solution.py:173
  304.6 10.5 %fusion.157 = f32[2048,512]{1,0:T(8,128)} fusion(bf16[2048,2048]{1,0:T(8,128)(2,1)} %get-tuple-element.34, bf16[2048,512]{1,0:T(8,128)(2,1)} %bitcast.342), kind=kOutput, calls=%fused_computation.241 | convolution fusion | flops 4294967296 | bytes 14680064 | tf_op jit(solution)/shard_map/nf,nd->fd/dot_general | solution.py:145
  315.1 32.0 %all-to-all-done.2 = bf16[8,4,32,1024]{3,1,0,2:T(4,128)(2,1)} async-done(((bf16[8,4,32,1024]{3,1,0,2:T(4,128)(2,1)}), bf16[8,4,32,1024]{3,1,0,2:T(4,128)(2,1)}, u32[]{:S(2)}, u32[]{:S(2)}) %all-to-all-start.2) | async-done | bytes 2097184 | tf_op jit(solution)/shard_map/all_to_all | solution.py:173
  350.8 4.5 reshape.461
  355.3 4.8 fusion.64
  363.0 5.3 reshape.462
  379.2 4.9 copy.157
  384.1 5.2 reshape.463
  389.2 6.5 fusion.68
  399.2 7.0 %reshape.498 = bf16[8,64,2,1024]{3,2,0,1:T(2,128)(2,1)} reshape(bf16[8,64,2,2,512]{4,3,2,0,1:T(2,128)(2,1)} %copy.207) | data formatting | bytes 4194304 | tf_op jit(solution)/shard_map/convert_element_type | solution.py:201
  406.2 9.7 %all-to-all-start.3 = ((bf16[8,64,2,1024]{3,2,0,1:T(2,128)(2,1)}), bf16[8,64,2,1024]{3,2,0,1:T(2,128)(2,1)}, u32[]{:S(2)}, u32[]{:S(2)}) async-start(bf16[8,64,2,1024]{3,2,0,1:T(2,128)(2,1)} %reshape.498), calls=%async_computation.3 | async-start | bytes 4194304 | tf_op jit(solution)/shard_map/all_to_all | solution.py:204
  416.2 10.7 %fusion.156 = f32[512,2048]{1,0:T(8,128)} fusion(bf16[2048,512]{1,0:T(8,128)(2,1)} %bitcast.344, bf16[2048,2048]{1,0:T(8,128)(2,1)} %get-tuple-element.66), kind=kOutput, calls=%fused_computation.240 | convolution fusion | flops 4294967296 | bytes 14680064 | tf_op jit(solution)/shard_map/nd,nf->df/dot_general | solution.py:151
  430.5 38.6 %all-to-all-done.3 = bf16[8,64,2,1024]{3,2,0,1:T(2,128)(2,1)} async-done(((bf16[8,64,2,1024]{3,2,0,1:T(2,128)(2,1)}), bf16[8,64,2,1024]{3,2,0,1:T(2,128)(2,1)}, u32[]{:S(2)}, u32[]{:S(2)}) %all-to-all-start.3) | async-done | bytes 2097184 | tf_op jit(solution)/shard_map/all_to_all | solution.py:204
  477.2 5.7 fusion.18
  488.2 52.8 %all-reduce = (f32[512]{0:T(512)}, f32[512]{0:T(512)}, f32[2,512]{1,0:T(2,128)}, f32[2,512]{1,0:T(2,128)}, f32[512]{0:T(512)}, /*index=5*/f32[512]{0:T(512)}, f32[2048]{0:T(1024)}, f32[512]{0:T(512)}) all-reduce(f32[512]{0:T(512)S(1)} %get-tuple-element.14, ...), channel_id=1, replica_groups=mesh['batch'=2,'grid'=16] {'batch','grid'}, use_global_device_ids=true, to_apply=%region_9.10 | all-reduce | flops 6656 | bytes 53248 | tf_op jit(solution)/shard_map/psum | solution.py:217
  541.0 7.1 %add_add_fusion.2 = f32[8,4,64,512]{3,2,1,0:T(8,128)} fusion(f32[8,4,64,512]{3,2,1,0:T(8,128)} %get-tuple-element.38, bf16[8,4,64,512]{3,2,1,0:T(8,128)(2,1)} %param.18, f32[8,4,64]{2,1,0:T(4,128)S(1)} %negate_multiply_fusion.2, f32[8,4,64]{2,1,0:T(4,128)S(1)} %negate_multiply_fusion.3, f32[8]{0:T(128)S(1)} %copy-done.54, ...), kind=kLoop, calls=%fused_computation.44 | loop fusion | flops 13631488 | bytes 16820256 | tf_op jit(solution)/shard_map/add | solution.py:208
  548.1 98.5 %all-reduce.4.cloned.1.call-done = (f32[2,8,64,64]{3,2,1,0:T(8,128)}, f32[2,8,64,64]{3,2,1,0:T(8,128)}, f32[512,2048]{1,0:T(8,128)}, f32[2048,512]{1,0:T(8,128)}) async-done(((f32[2,8,64,64]{3,2,1,0:T(8,128)}, f32[2,8,64,64]{3,2,1,0:T(8,128)}, f32[512,2048]{1,0:T(8,128)}, f32[2048,512]{1,0:T(8,128)}), (f32[2,8,64,64]{3,2,1,0:T(8,128)}, f32[2,8,64,64]{3,2,1,0:T(8,128)}, f32[512,2048]{1,0:T(8,128)}, ...) | async-done | bytes 8912912 | tf_op jit(solution)/shard_map/psum | solution.py:217
  650.4 4.8 copy.278
  (221 shorter events, 120.5 us)
Async XLA Ops:
  7.2 186.4 %copy-start = (bf16[512,2048]{1,0:T(8,128)(2,1)S(1)}, bf16[512,2048]{1,0:T(8,128)(2,1)}, u32[]{:S(2)}) copy-start(bf16[512,2048]{1,0:T(8,128)(2,1)} %param.30) | copy-start | bytes 6291460
  7.3 177.3 %copy-start.24 = (f32[64,1,32]{0,2,1:T(8,128)}, f32[64,1,32]{0,2,1:T(8,128)S(1)}, u32[]{:S(2)}) copy-start(f32[64,1,32]{0,2,1:T(8,128)S(1)} %get-tuple-element.67) | copy-start | bytes 24580
  7.3 177.3 %copy-start.26 = (f32[64,1,32]{0,2,1:T(8,128)}, f32[64,1,32]{0,2,1:T(8,128)S(1)}, u32[]{:S(2)}) copy-start(f32[64,1,32]{0,2,1:T(8,128)S(1)} %get-tuple-element.68) | copy-start | bytes 24580
  20.6 13.0 %copy-start.57 = (f32[2,512]{1,0:T(2,128)S(1)}, f32[2,512]{1,0:T(2,128)}, u32[]{:S(2)}) copy-start(f32[2,512]{1,0:T(2,128)} %param.25) | copy-start | bytes 12292
  20.6 13.1 %copy-start.58 = (f32[2,512]{1,0:T(2,128)S(1)}, f32[2,512]{1,0:T(2,128)}, u32[]{:S(2)}) copy-start(f32[2,512]{1,0:T(2,128)} %param.27) | copy-start | bytes 12292
  20.6 13.2 %copy-start.32 = (bf16[2,8,64,64]{3,2,1,0:T(8,128)(2,1)S(1)}, bf16[2,8,64,64]{3,2,1,0:T(8,128)(2,1)}, u32[]{:S(2)}) copy-start(bf16[2,8,64,64]{3,2,1,0:T(8,128)(2,1)} %param.24) | copy-start | bytes 393220
  20.6 13.5 %copy-start.33 = (bf16[2,8,64,64]{3,2,1,0:T(8,128)(2,1)S(1)}, bf16[2,8,64,64]{3,2,1,0:T(8,128)(2,1)}, u32[]{:S(2)}) copy-start(bf16[2,8,64,64]{3,2,1,0:T(8,128)(2,1)} %param.26) | copy-start | bytes 393220
  25.0 51.6 %all-to-all-start = ((bf16[8,4,32,1024]{3,1,0,2:T(4,128)(2,1)}), bf16[8,4,32,1024]{3,1,0,2:T(4,128)(2,1)}, u32[]{:S(2)}, u32[]{:S(2)}) async-start(bf16[8,4,32,1024]{3,1,0,2:T(4,128)(2,1)} %reshape.495), calls=%async_computation | async-start | bytes 4194304 | tf_op jit(solution)/shard_map/all_to_all | solution.py:116
  33.7 59.2 %copy-start.51 = (f32[2,8,64]{2,0,1:T(2,128)}, f32[2,8,64]{2,0,1:T(2,128)S(1)}, u32[]{:S(2)}) copy-start(f32[2,8,64]{2,0,1:T(2,128)S(1)} %copy.139) | copy-start | bytes 12292
  33.8 68.0 %copy-start.44 = (f32[2,8,64]{2,0,1:T(2,128)}, f32[2,8,64]{2,0,1:T(2,128)S(1)}, u32[]{:S(2)}) copy-start(f32[2,8,64]{2,0,1:T(2,128)S(1)} %copy.140) | copy-start | bytes 12292
  34.6 76.9 %copy-start.16 = (f32[32,1,64,2]{2,0,3,1:T(8,128)}, f32[32,1,64,2]{2,0,3,1:T(8,128)S(1)}, u32[]{:S(2)}) copy-start(f32[32,1,64,2]{2,0,3,1:T(8,128)S(1)} %get-tuple-element.48) | copy-start | bytes 49156
  34.6 76.8 %copy-start.18 = (f32[32,1,64,2]{2,0,3,1:T(8,128)}, f32[32,1,64,2]{2,0,3,1:T(8,128)S(1)}, u32[]{:S(2)}) copy-start(f32[32,1,64,2]{2,0,3,1:T(8,128)S(1)} %get-tuple-element.49) | copy-start | bytes 49156
  35.4 57.5 %copy-start.11 = (bf16[8,1,64,2,64]{2,4,1,3,0:T(8,128)(2,1)}, bf16[8,1,64,2,64]{2,4,1,3,0:T(8,128)(2,1)S(1)}, u32[]{:S(2)}) copy-start(bf16[8,1,64,2,64]{2,4,1,3,0:T(8,128)(2,1)S(1)} %get-tuple-element.46) | copy-start | bytes 393220
  92.9 9.8 %copy-start.28 = (bf16[8,1,64,2,64]{2,4,1,3,0:T(8,128)(2,1)S(1)}, bf16[8,1,64,2,64]{2,4,1,3,0:T(8,128)(2,1)}, u32[]{:S(2)}) copy-start(bf16[8,1,64,2,64]{2,4,1,3,0:T(8,128)(2,1)} %get-tuple-element.44) | copy-start | bytes 393220
  92.9 9.8 %copy-start.30 = (bf16[8,1,64,2,64]{2,4,1,3,0:T(8,128)(2,1)S(1)}, bf16[8,1,64,2,64]{2,4,1,3,0:T(8,128)(2,1)}, u32[]{:S(2)}) copy-start(bf16[8,1,64,2,64]{2,4,1,3,0:T(8,128)(2,1)} %get-tuple-element.45) | copy-start | bytes 393220
  116.7 17.5 %copy-start.65 = (s32[12]{0:T(128)S(1)}, s32[12]{0:T(128)}, u32[]{:S(2)}) copy-start(s32[12]{0:T(128)} %param.21) | copy-start | bytes 148
  116.7 17.5 %copy-start.66 = (s32[8]{0:T(128)S(1)}, s32[8]{0:T(128)}, u32[]{:S(2)}) copy-start(s32[8]{0:T(128)} %param.19) | copy-start | bytes 100
  116.8 17.7 %copy-start.63 = (s32[12,4]{0,1:T(4,128)S(1)}, s32[12,4]{0,1:T(4,128)}, u32[]{:S(2)}) copy-start(s32[12,4]{0,1:T(4,128)} %param.20) | copy-start | bytes 580
  123.8 52.9 %all-to-all-start.1 = ((bf16[8,64,2,1024]{3,2,0,1:T(2,128)(2,1)}), bf16[8,64,2,1024]{3,2,0,1:T(2,128)(2,1)}, u32[]{:S(2)}, u32[]{:S(2)}) async-start(bf16[8,64,2,1024]{3,2,0,1:T(2,128)(2,1)} %reshape.496), calls=%async_computation.1 | async-start | bytes 4194304 | tf_op jit(solution)/shard_map/all_to_all | solution.py:131
  134.3 50.4 %copy-start.55 = (f32[32]{0:T(128)}, f32[32]{0:T(128)S(1)}, u32[]{:S(2)}) copy-start(f32[32]{0:T(128)S(1)} %fusion.134) | copy-start | bytes 388
  134.5 45.7 %copy-start.53 = (f32[8]{0:T(128)}, f32[8]{0:T(128)S(1)}, u32[]{:S(2)}) copy-start(f32[8]{0:T(128)S(1)} %fusion.76) | copy-start | bytes 100
  134.8 49.9 %copy-start.38 = (f32[8,512]{1,0:T(8,128)}, f32[8,512]{1,0:T(8,128)S(1)}, u32[]{:S(2)}) copy-start(f32[8,512]{1,0:T(8,128)S(1)} %broadcast_bitcast_fusion) | copy-start | bytes 49156
  193.6 41.5 %copy-start.10 = (bf16[8,4,64,512]{3,2,1,0:T(8,128)(2,1)}, bf16[8,4,64,512]{3,2,1,0:T(8,128)(2,1)S(1)}, u32[]{:S(2)}) copy-start(bf16[8,4,64,512]{3,2,1,0:T(8,128)(2,1)S(1)} %add_convert_fusion.2) | copy-start | bytes 6291460
  294.3 52.8 %all-to-all-start.2 = ((bf16[8,4,32,1024]{3,1,0,2:T(4,128)(2,1)}), bf16[8,4,32,1024]{3,1,0,2:T(4,128)(2,1)}, u32[]{:S(2)}, u32[]{:S(2)}) async-start(bf16[8,4,32,1024]{3,1,0,2:T(4,128)(2,1)} %reshape.497), calls=%async_computation.2 | async-start | bytes 4194304 | tf_op jit(solution)/shard_map/all_to_all | solution.py:173
  347.1 8.2 %copy-start.17 = (f32[32,1,64,2]{2,0,3,1:T(8,128)S(1)}, f32[32,1,64,2]{2,0,3,1:T(8,128)}, u32[]{:S(2)}) copy-start(f32[32,1,64,2]{2,0,3,1:T(8,128)} %copy-done.16) | copy-start | bytes 49156
  347.1 8.2 %copy-start.19 = (f32[32,1,64,2]{2,0,3,1:T(8,128)S(1)}, f32[32,1,64,2]{2,0,3,1:T(8,128)}, u32[]{:S(2)}) copy-start(f32[32,1,64,2]{2,0,3,1:T(8,128)} %copy-done.18) | copy-start | bytes 49156
  406.2 62.9 %all-to-all-start.3 = ((bf16[8,64,2,1024]{3,2,0,1:T(2,128)(2,1)}), bf16[8,64,2,1024]{3,2,0,1:T(2,128)(2,1)}, u32[]{:S(2)}, u32[]{:S(2)}) async-start(bf16[8,64,2,1024]{3,2,0,1:T(2,128)(2,1)} %reshape.498), calls=%async_computation.3 | async-start | bytes 4194304 | tf_op jit(solution)/shard_map/all_to_all | solution.py:204
  416.0 230.7 %all-reduce.4.cloned.1.call-start = ((), (), s32[]{:S(2)}) async-start(), calls=%async_computation.4 | async-start | bytes 18874368 | tf_op jit(solution)/shard_map/psum | solution.py:217
  416.2 10.8 %copy-start.8 = (bf16[512,2,8,64]{0,3,1,2:T(8,128)(2,1)S(1)}, bf16[512,2,8,64]{0,3,1,2:T(8,128)(2,1)}, u32[]{:S(2)}) copy-start(bf16[512,2,8,64]{0,3,1,2:T(8,128)(2,1)} %copy-done.7) | copy-start | bytes 3145732
  416.2 10.8 %copy-start.15 = (bf16[512,2,8,64]{0,3,1,2:T(8,128)(2,1)S(1)}, bf16[512,2,8,64]{0,3,1,2:T(8,128)(2,1)}, u32[]{:S(2)}) copy-start(bf16[512,2,8,64]{0,3,1,2:T(8,128)(2,1)} %copy-done.14) | copy-start | bytes 3145732
  469.2 8.0 %copy-start.21 = (f32[8,4,64]{2,1,0:T(4,128)S(1)}, f32[8,4,64]{2,1,0:T(4,128)}, u32[]{:S(2)}) copy-start(f32[8,4,64]{2,1,0:T(4,128)} %copy-done.20) | copy-start | bytes 24580
  469.2 8.0 %copy-start.49 = (f32[512]{0:T(512)S(1)}, f32[512]{0:T(512)}, u32[]{:S(2)}) copy-start(f32[512]{0:T(512)} %param.22) | copy-start | bytes 6148
  (43 other events, 139.2 us)
Sparse Core Ops, SparseCore 0:
  430.5 216.0 all-reduce.3
where the time goes:
time: 671 us; the launch traced here: 664 us
  waiting for transfers between devices  247 us (37%)
  matrix products  153 us (23%)
  local copies, waits for them, and re-layouts  122 us (18%)
  blocking collectives  52.8 us (8%)
  starting transfers between devices  39.2 us (6%)
  other arithmetic  35.2 us (5%)
  between operations  15.2 us (2%)
    psum x1, waiting for transfers between devices, local(): summed = tuple(lax.psum(mixer_grads + mlp_grads, ('batch', 'grid')))  98.5 us
    psum x1, blocking collectives, local(): summed = tuple(lax.psum(mixer_grads + mlp_grads, ('batch', 'grid')))  52.8 us
    dot_general x1, matrix products, local(): jnp.dot(normed_two_bf, mlp_in, preferred_element_type=jnp.float32)  41.5 us
    all_to_all x1, waiting for transfers between devices, local(): lax.all_to_all(col_spec, 'grid', split_axis=2, concat_axis=1, tiled=True)  40.3 us
    all_to_all x1, waiting for transfers between devices, local(): lax.all_to_all(grad_col_spec, 'grid', split_axis=1, concat_axis=2, tiled=...  38.6 us
    all_to_all x1, waiting for transfers between devices, local(): lax.all_to_all(row_back, 'grid', split_axis=1, concat_axis=2, tiled=True)  37.5 us
    all_to_all x1, waiting for transfers between devices, local(): lax.all_to_all(grad_back, 'grid', split_axis=2, concat_axis=1, tiled=True)  32 us
    dot_general x1, matrix products, local(): jnp.einsum('nd,fd->nf', grad_branch, mlp_out, preferred_element_type=jnp....  21.8 us
  transfers between devices with their start and end apart: 5, of which 5 were waited for; matrix products, arithmetic and copies ran while one was open for 8% of the time, Pallas kernels for 0%

commit v1 on v0

v1 whole, which is shorter than its diff:
```python
import functools
import math

import jax
import jax.numpy as jnp
import numpy as np
from jax import lax
from jax.experimental import pallas as pl
from jax.experimental.pallas import tpu as pltpu
from jax.sharding import PartitionSpec as P

BLOCKS = 8
MODES = 32
BSIZE = 64
EPSILON = 1e-06
SHRINK = 0.1
MESH = pl.DeviceIdType.MESH
F32 = jnp.float32
BF16 = jnp.bfloat16
CELLS = 512
TILE = 16
COPY = 32
FT = 512


def sizes_of(items, rows, cols, feats, hidden, grid):
    sz = type("Sizes", (), {})()
    sz.items, sz.rows, sz.cols, sz.feats, sz.hidden, sz.grid = items, rows, cols, feats, hidden, grid
    sz.own = MODES // grid
    sz.height = rows * grid
    sz.item_cells = rows * cols
    sz.sub_items = 16 // (rows * sz.own * 2)
    sz.sub_cells = sz.sub_items * sz.item_cells
    sz.subs = CELLS // sz.sub_cells
    sz.chunk_items = sz.subs * sz.sub_items
    sz.chunks = items // sz.chunk_items
    sz.sub_modes = sz.sub_items * sz.own * MODES
    sz.modes = sz.subs * sz.sub_modes
    return sz


def halves(table):
    high = table.astype(BF16)
    low = (table - high.astype(np.float64)).astype(BF16)
    return np.stack([high, low])


def tables(sz):
    its, rows, own, cols, grid = sz.sub_items, sz.rows, sz.own, sz.cols, sz.grid
    w = np.arange(cols)
    q = np.arange(MODES)
    angle = 2 * np.pi * (np.outer(q, w) % cols) / cols
    col = np.stack([np.cos(angle), -np.sin(angle)], axis=1) / math.sqrt(cols)
    lines = its * rows
    eye = np.eye(lines)

    def placed(tab):
        tab = tab.reshape(grid, own, 2, cols)
        big = np.einsum("gqrw,lm->glqrmw", tab, eye)
        return big.reshape(grid * 16, lines * cols)

    first = placed(col)
    p = np.where(q < MODES // 2, q, sz.height - MODES + q)
    h = np.arange(sz.height)
    angle = 2 * np.pi * (np.outer(p, h) % sz.height) / sz.height
    cosine, sine = np.cos(angle), np.sin(angle)
    row = np.stack([np.stack([cosine, sine], -1), np.stack([-sine, cosine], -1)], 1) / math.sqrt(sz.height)
    row = row.reshape(MODES, 2, grid, rows, 2)
    big = np.einsum("psghr,ij,qk->siqpgjhkr", row, np.eye(its), np.eye(own))
    big = big.reshape(2 * sz.sub_modes, grid * 16)
    return [halves(t) for t in (first, first.T, big, big.T)]


def dot(a, b):
    return jnp.dot(a, b, preferred_element_type=F32)


def dot_nt(a, b):
    return lax.dot_general(a, b, (((1,), (1,)), ((), ())), preferred_element_type=F32)


def dot_tn(a, b):
    return lax.dot_general(a, b, (((0,), (0,)), ((), ())), preferred_element_type=F32)


def split(v):
    high = v.astype(BF16)
    return high, (v - high.astype(F32)).astype(BF16)


CDF = (
    0.797884941492634, 0.03633308439449127, -3.259472654998994e-05, -5.530632529808752e-05, 3.964774886835927e-06,
    -1.3226642974616402e-07, 1.756281964154736e-09,
)


def gelu_parts(v):
    square = v * v
    inner = jnp.minimum(square, 30.0)
    q = CDF[6] * inner + CDF[5]
    for coef in CDF[4::-1]:
        q = q * inner + coef
    cdf = 0.5 + 0.5 * jnp.tanh(v * q)
    pdf = jnp.exp2(square * (-0.5 * math.log2(math.e))) * (1.0 / math.sqrt(2.0 * math.pi))
    return v * cdf, cdf + v * pdf


def moments(v):
    centred = v - jnp.mean(v, axis=-1, keepdims=True)
    scale = lax.rsqrt(jnp.mean(centred * centred, axis=-1, keepdims=True) + EPSILON)
    return centred * scale, scale


def pull_norm(grad, xhat, scale, gain):
    gy = grad * gain
    return (gy - jnp.mean(gy, -1, keepdims=True) - xhat * jnp.mean(gy * xhat, -1, keepdims=True)) * scale


def eight_rows(v):
    return jnp.sum(v.reshape(v.shape[0] // 8, 8, v.shape[1]), axis=0)


GAIN1, BIAS1, SB1, SB2, GAIN2, BIAS2, BOUT, BIN = 0, 1, 2, 4, 6, 7, 8, 9


def tiled(count, body):
    size = min(count, COPY)

    @pl.loop(0, count // size, unroll=min(4, count // size))
    def _(t):
        body(t * size, size)


def each_tile(rows):
    return pl.loop(0, rows // TILE, unroll=rows // TILE)


def landing_rows(rows, bits):
    total = 0
    for _ in range(bits):
        rows = rows // 2 if rows % 32 == 0 else rows
        total += rows
    return total


class Pieces:
    def __init__(self, source, target, rows, send_sem, recv_sem, device):
        self.source, self.target, self.rows, self.device = source, target, rows, device
        self.send_sem, self.recv_sem = send_sem, recv_sem

    def part(self, at):
        return pltpu.make_async_remote_copy(
            src_ref=self.source.at[at], dst_ref=self.target.at[at], send_sem=self.send_sem, recv_sem=self.recv_sem,
            device_id=self.device, device_id_type=MESH,
        )

    def start(self):
        size = max(16, self.rows // 8)

        @pl.loop(0, self.rows // size)
        def _(k):
            self.part(pl.ds(pl.multiple_of(k * size, 16), size)).start()

    def wait_send(self):
        self.part(pl.ds(0, self.rows)).wait_send()

    def wait_recv(self):
        self.part(pl.ds(0, self.rows)).wait_recv()


class Reducer:
    def __init__(self, acc, stages, landing, near, send_sems, recv_sems, order, index):
        self.acc, self.stages, self.landing, self.near = acc, stages, landing, near
        self.send_sems, self.recv_sems = send_sems, recv_sems
        self.steps = []
        size, off, land = acc.shape[0], 0, 0
        for axis, bit in order:
            side = lax.rem(index[axis] // 2**bit, 2)
            partner = {axis: index[axis] + (1 - 2 * side) * 2**bit}
            halving = size % 32 == 0
            if halving:
                size = size // 2
                away, off = off + (1 - side) * size, off + side * size
            else:
                away = off
            self.steps.append((halving, size, away, off, land, partner))
            land += size
        self.off, self.size = off, size
        self.back = [k for k in reversed(range(1, len(order))) if self.steps[k][0]]

    def at(self, off, size):
        return pl.ds(pl.multiple_of(off, 16), size)

    def stage(self, k):
        halving, size, away, off, land, partner = self.steps[k]
        if not halving:
            return self.near(off - self.steps[0][3], size)
        return self.stages[0] if k == 0 else self.stages[1].at[pl.ds(land - self.steps[0][1], size)]

    def copy(self, k):
        halving, size, away, off, land, partner = self.steps[k]
        return Pieces(
            self.stage(k), self.landing.at[pl.ds(land, size)], size, self.send_sems.at[k], self.recv_sems.at[k], partner
        )

    def start(self, k):
        halving, size, away, off, land, partner = self.steps[k]

        stage = self.stage(k)

        def body(o, n):
            stage[pl.ds(o, n), :] = self.acc[self.at(away + o, n), :].astype(BF16)

        tiled(size, body)
        self.copy(k).start()

    def finish(self, k):
        halving, size, away, off, land, partner = self.steps[k]
        self.copy(k).wait_recv()
        if not halving:
            self.copy(k).wait_send()
        stage = self.stage(k)

        def body(o, n):
            at = self.at(off + o, n)
            mine = self.acc[at, :] if halving else stage[pl.ds(o, n), :].astype(F32)
            self.acc[at, :] = mine + self.landing[pl.ds(land + o, n), :].astype(F32)

        tiled(size, body)

    def begin_back(self):
        first = self.steps[0][3]

        def body(o, n):
            at = self.at(self.off + o, n)
            self.near(self.off - first + o, n)[...] = self.acc[at, :].astype(BF16)

        tiled(self.size, body)

    def back_copy(self, i):
        halving, size, away, off, land, partner = self.steps[self.back[i]]
        part = self.near(off - self.steps[0][3], size)
        sem = len(self.steps) + i
        return Pieces(part, part, size, self.send_sems.at[sem], self.recv_sems.at[sem], partner)

    def ticks(self):
        count, back = len(self.steps), len(self.back)

        def first():
            self.start(0)

        def forth(k):
            self.finish(k)
            if k + 1 < count:
                self.start(k + 1)
            else:
                self.begin_back()
                self.back_copy(0).start()

        def home(i):
            self.back_copy(i).wait_recv()
            if i + 1 < back:
                self.back_copy(i + 1).start()

        return (
            [first]
            + [functools.partial(forth, k) for k in range(count)]
            + [functools.partial(home, i) for i in range(back)]
        )

    def wait_sent(self):
        for k, step in enumerate(self.steps):
            if step[0]:
                self.copy(k).wait_send()
        for i in range(len(self.back)):
            self.back_copy(i).wait_send()


def kernel(
    sz, batch_bits, grid_bits,
    ids, masks, counts,
    x_hbm, cot_hbm, gain1, bias1, gain2, bias2, sw1, sb1, sw2, sb2, b_in, b_out,
    t_f, t_b, t_rf, t_rb, win_hbm, wout_hbm,
    act_hbm, ig_hbm, near_hbm, dspec_out, dvec_out,
    x_v, cot_v, w_in, w_out, send_a, recv_a, send_b, recv_b, gres,
    spec, act1, slope1, slope2, w1, w2, dw1, dw2,
    n2, n2t, gb, gbt, act_s, gh_s, live, weight,
    dm_acc, dm_land, late_acc, late_stage, late_land, late_split, late_parts, late_near, late_far, dvec, sums, hid_s, pul_s, n1_send, n1_recv,
    sem_x, sem_cot, sem_w, sem_out, sem_ig, sem_dm, send_sems, recv_sems,
    dm_send, dm_recv, late_send, late_recv, n1_ssem, n1_rsem,
):
    grid, feats = sz.grid, sz.feats
    chunks, subs = sz.chunks, sz.subs
    me = lax.axis_index("grid")
    index = {"batch": lax.axis_index("batch"), "grid": me}
    hi_v, lo_v = n2, gb
    modes = sz.modes
    groups = feats // 128
    mix_rows = 4 * groups * BSIZE
    blocks = sz.hidden // FT
    order = [("batch", b) for b in range(batch_bits)] + [("grid", b) for b in range(grid_bits)]
    swapped = list(order)
    if grid_bits > 1:
        swapped[batch_bits], swapped[batch_bits + 1] = swapped[batch_bits + 1], swapped[batch_bits]

    for c in range(chunks):
        pltpu.make_async_copy(x_hbm.at[c], x_v.at[c], sem_x.at[c]).start()
    for c in range(chunks):
        pltpu.make_async_copy(cot_hbm.at[c], cot_v.at[c], sem_cot.at[c]).start()
    load_win = pltpu.make_async_copy(win_hbm, w_in, sem_w.at[0])
    load_wout = pltpu.make_async_copy(wout_hbm, w_out, sem_w.at[1])
    load_win.start()
    load_wout.start()

    barrier = pltpu.get_barrier_semaphore()

    def other(k):
        batch = 2**batch_bits
        b = lax.rem(index["batch"] + k // grid, batch)
        g = lax.rem(me + lax.rem(k, grid), grid)
        return {"batch": b, "grid": g}

    everyone = 2**batch_bits * grid
    my_place = index["batch"] * grid + me

    @pl.loop(1, everyone)
    def _(k):
        pl.semaphore_signal(barrier, inc=1, device_id=other(k), device_id_type=MESH)

    def exchange(stage, c, send, recv):
        @pl.loop(0, grid - 1)
        def _(j):
            k = grid // 2 + ((j + 1) // 2) * (2 * lax.rem(j + 1, 2) - 1)
            peer = lax.rem(me + k, grid)
            pltpu.make_async_remote_copy(
                src_ref=send.at[c, :, peer],
                dst_ref=recv.at[c, :, me],
                send_sem=send_sems.at[stage, c],
                recv_sem=recv_sems.at[stage, c],
                device_id={"grid": peer},
                device_id_type=MESH,
            ).start()

        for s in range(subs):
            recv[c, s, me] = send[c, s, me]

    def arrived(stage, c, recv):
        part = recv.at[c, :, pl.ds(0, grid - 1)]
        pltpu.make_async_copy(part, part, recv_sems.at[stage, c]).wait()

    def sent(stage, c, send):
        part = send.at[c, :, pl.ds(0, grid - 1)]
        pltpu.make_async_copy(part, part, send_sems.at[stage, c]).wait()

    def doubled(rows, inner):
        mode = lax.rem(lax.broadcasted_iota(jnp.int32, (rows, 1), 0) // inner, sz.own)
        return jnp.where(mode + me * sz.own == 0, 1.0, 2.0).astype(F32)

    def row_tile(t):
        return pl.ds(pl.multiple_of(t * TILE, TILE), TILE)

    def mix_tile(j, t):
        return pl.ds(pl.multiple_of(j * sz.modes + t * TILE, TILE), TILE)

    def lanes(j):
        return pl.ds(128 * j, 128)

    def wide(j):
        return pl.ds(256 * j, 256)

    def send_columns(c, table, send):
        for s in range(subs):
            cells = pl.ds(s * sz.sub_cells, sz.sub_cells)
            high = hi_v[cells, :]
            out = dot(table[0], high) + dot(table[0], lo_v[cells, :]) + dot(table[1], high)
            send[c, s] = out.astype(BF16).reshape(grid, 16, feats)

    def both_parts(ref, j):
        return jnp.concatenate([ref[0, :, lanes(j)], ref[1, :, lanes(j)]], axis=1)

    def bias_parts(ref, j):
        return jnp.concatenate([ref[0:1, lanes(j)], ref[1:2, lanes(j)]], axis=1)

    @pl.loop(0, chunks)
    def _(c):
        pltpu.make_async_copy(x_hbm.at[c], x_v.at[c], sem_x.at[c]).wait()

        @each_tile(CELLS)
        def _(t):
            xhat, scale = moments(x_v[c, row_tile(t), :].astype(F32))
            hi_v[row_tile(t), :], lo_v[row_tile(t), :] = split(xhat * gain1[...] + bias1[...])

        send_columns(c, t_f, send_a)

        @pl.when(c == 0)
        def _():
            pl.semaphore_wait(barrier, everyone - 1)

        exchange(0, c, send_a, recv_a)


    pick_row = lax.broadcasted_iota(jnp.int32, (BSIZE, 128), 0)
    pick_lane = lax.broadcasted_iota(jnp.int32, (BSIZE, 128), 1)
    picks = [(pick_lane == pick_row + BSIZE * side).astype(F32).astype(BF16) for side in range(2)]
    for raw, big in ((sw1, w1), (sw2, w2)):
        for j in range(groups):
            real, imag = [
                jnp.concatenate([dot(raw[r, 2 * j + side], picks[side]) for side in range(2)], axis=0) for r in range(2)
            ]
            big[j, :128, :128] = real.astype(BF16)
            big[j, :128, 128:] = imag.astype(BF16)
            big[j, 128:, :128] = (-imag).astype(BF16)
            big[j, 128:, 128:] = real.astype(BF16)

    width = feats // masks.shape[0]

    @pl.loop(0, sz.items)
    def _(i):
        kind = ids[i]
        for g in range(masks.shape[0]):
            live[i, :, pl.ds(g * width, width)] = jnp.full((1, width), masks[g, kind].astype(F32))
        weight[i] = jnp.full((1, feats), counts[kind].astype(F32) * 0.125)

    for s in range(dm_acc.shape[0]):

        def clear(o, n):
            dm_acc[s, pl.ds(o, n), :] = jnp.zeros((n, feats), F32)

        tiled(dm_acc.shape[1], clear)
    dw1[...] = jnp.zeros_like(dw1)
    dw2[...] = jnp.zeros_like(dw2)
    dvec[...] = jnp.zeros_like(dvec)
    sums[...] = jnp.zeros_like(sums)

    @pl.loop(0, chunks)
    def _(c):
        arrived(0, c, recv_a)
        for s in range(subs):
            got = recv_a[c, s].reshape(grid * 16, feats)
            out = (dot(t_rf[0], got) + dot(t_rf[1], got)).astype(BF16)
            at = pl.ds(s * sz.sub_modes, sz.sub_modes)
            spec[c, 0, at, :] = out[: sz.sub_modes]
            spec[c, 1, at, :] = out[sz.sub_modes :]
        for j in range(groups):
            pul_s[pl.ds(j * sz.modes, sz.modes), :256] = dot(both_parts(spec.at[c], j), w1[j])
        for j in range(groups):

            @each_tile(sz.modes)
            def _(t):
                at = row_tile(t)
                act, slope = gelu_parts(pul_s[mix_tile(j, t), :256] + bias_parts(sb1, j))
                act1[c, at, wide(j)] = act.astype(BF16)
                slope1[c, at, wide(j)] = slope

        for j in range(groups):
            pul_s[pl.ds(j * sz.modes, sz.modes), :256] = dot(act1[c, :, wide(j)], w2[j])
        for j in range(groups):

            @each_tile(sz.modes)
            def _(t):
                at = row_tile(t)
                mixed = pul_s[mix_tile(j, t), :256] + bias_parts(sb2, j)
                bend = jnp.tanh(mixed * (1.0 / SHRINK))
                slope2[c, at, wide(j)] = bend * bend
                shrunk = (mixed - SHRINK * bend).astype(BF16)
                gbt[mix_tile(0, t), lanes(j)] = shrunk[:, :128]
                gbt[mix_tile(1, t), lanes(j)] = shrunk[:, 128:]

        for s in range(subs):
            at = pl.ds(s * sz.sub_modes, sz.sub_modes)
            second, third, fourth = [pl.ds(k * modes + s * sz.sub_modes, sz.sub_modes) for k in (1, 2, 3)]
            high = jnp.concatenate([gbt[at, :], gbt[second, :]], axis=0)
            out = (dot(t_rb[0], high) + dot(t_rb[1], high)) * doubled(grid * 16, 2)
            send_b[c, s] = out.astype(BF16).reshape(grid, 16, feats)
        exchange(1, c, send_b, recv_b)

    load_win.wait()
    load_wout.wait()

    def feed_forward(c):
        pltpu.make_async_copy(cot_hbm.at[c], cot_v.at[c], sem_cot.at[c]).wait()
        arrived(1, c, recv_b)
        for s in range(subs):
            cells = pl.ds(s * sz.sub_cells, sz.sub_cells)
            got = recv_b[c, s].reshape(grid * 16, feats)
            gres[c, cells, :] = dot(t_b[0], got) + dot(t_b[1], got)

        @each_tile(CELLS)
        def _(t):
            at = row_tile(t)
            item = c * sz.chunk_items + (t * TILE) // sz.item_cells
            total = x_v[c, at, :].astype(F32) + live[item] * gres[c, at, :]
            gres[c, at, :] = total
            xhat, scale = moments(total)
            n2[at, :] = (xhat * gain2[...] + bias2[...]).astype(BF16)
            grad = (cot_v[c, at, :].astype(F32) * weight[item]).astype(BF16)
            gb[at, :] = grad
            sums[BOUT] += eight_rows(grad.astype(F32))

        n2t[...] = n2[...].T
        gbt[...] = gb[...].T

        def products(f):
            at = pl.ds(f * FT, FT)
            hid_s[...] = dot(n2[...], w_in[:, at])
            pul_s[...] = dot_nt(gb[...], w_out[at, :])

        for f in range(blocks):
            products(f)
            at = pl.ds(f * FT, FT)

            @each_tile(CELLS)
            def _(t):
                rows = row_tile(t)
                act, slope = gelu_parts(hid_s[rows, :] + b_in[:, at])
                act_s[rows, at] = act.astype(BF16)
                grad = (slope * pul_s[rows, :]).astype(BF16)
                gh_s[rows, at] = grad
                sums[BIN + f] += eight_rows(grad.astype(F32))

        hid_s[...] = dot_nt(gh_s[...], w_in[...])
        pul_s[...] = dot(act_s[...], w_out[...])

        @each_tile(CELLS)
        def _(t):
            at = row_tile(t)
            item = c * sz.chunk_items + (t * TILE) // sz.item_cells
            total = gres[c, at, :]
            xhat, scale = moments(total)
            grad = hid_s[at, :]
            sums[GAIN2] += eight_rows(grad * xhat)
            sums[BIAS2] += eight_rows(grad)
            grad_out = cot_v[c, at, :].astype(F32) * weight[item]
            cot_v[c, at, :] = (total + pul_s[at, :] + b_out[...]).astype(BF16)
            out = grad_out + pull_norm(grad, xhat, scale, gain2[...])
            gres[c, at, :] = out
            hi_v[at, :], lo_v[at, :] = split(out * live[item])

        sent(0, c, send_a)
        send_columns(c, t_f, send_a)
        exchange(2, c, send_a, recv_a)
        pltpu.make_async_copy(cot_v.at[c], act_hbm.at[c], sem_out.at[c]).start()
        for f in range(blocks):
            at, into = pl.ds(f * FT, FT), pl.ds((f % 2) * feats, feats)
            dm_acc[f // 2, into, :] += dot(n2t[...], gh_s[:, at])
            dm_acc[blocks // 2 + f // 2, into, :] += dot(gbt[...], act_s[:, at])

    def dz_of(j):
        return n2t[pl.ds((j // 2) * modes, modes), wide(j % 2)]

    def dm_of(j):
        return n2t[pl.ds((2 + j // 2) * modes, modes), wide(j % 2)]

    def mix_backward(c):
        arrived(2, c, recv_a)
        for s in range(subs):
            got = recv_a[c, s].reshape(grid * 16, feats)
            out = (dot(t_rf[0], got) + dot(t_rf[1], got)) * doubled(2 * sz.sub_modes, MODES)
            at = pl.ds(s * sz.sub_modes, sz.sub_modes)
            hid_s[at, :] = out[: sz.sub_modes]
            hid_s[pl.ds(sz.modes + s * sz.sub_modes, sz.sub_modes), :] = out[sz.sub_modes :]
        for j in range(groups):

            @each_tile(sz.modes)
            def _(t):
                at = row_tile(t)
                low_at = pl.ds(pl.multiple_of(sz.modes + t * TILE, TILE), TILE)
                both = jnp.concatenate([hid_s[at, lanes(j)], hid_s[low_at, lanes(j)]], axis=1)
                dz = (both * slope2[c, at, wide(j)]).astype(BF16)
                n2t[mix_tile(j // 2, t), wide(j % 2)] = dz
                dz = eight_rows(dz.astype(F32))
                for r in range(2):
                    sums[SB2 + r, :, lanes(j)] += dz[:, 128 * r : 128 * r + 128]

        for j in range(groups):
            pul_s[pl.ds(j * sz.modes, sz.modes), :256] = dot_nt(dz_of(j), w2[j])
        for j in range(groups):

            @each_tile(sz.modes)
            def _(t):
                at = row_tile(t)
                dm = (pul_s[mix_tile(j, t), :256] * slope1[c, at, wide(j)]).astype(BF16)
                n2t[mix_tile(2 + j // 2, t), wide(j % 2)] = dm
                dm = eight_rows(dm.astype(F32))
                for r in range(2):
                    sums[SB1 + r, :, lanes(j)] += dm[:, 128 * r : 128 * r + 128]

        for j in range(groups):
            pul_s[pl.ds(j * sz.modes, sz.modes), :256] = dot_nt(dm_of(j), w1[j])
        for j in range(groups):

            @each_tile(sz.modes)
            def _(t):
                at = row_tile(t)
                high, low = split(pul_s[mix_tile(j, t), :256])
                for r in range(2):
                    gbt[mix_tile(r, t), lanes(j)] = high[:, 128 * r : 128 * r + 128]
                    gbt[mix_tile(2 + r, t), lanes(j)] = low[:, 128 * r : 128 * r + 128]

        sent(1, c, send_b)
        for s in range(subs):
            at = pl.ds(s * sz.sub_modes, sz.sub_modes)
            second, third, fourth = [pl.ds(k * modes + s * sz.sub_modes, sz.sub_modes) for k in (1, 2, 3)]
            high = jnp.concatenate([gbt[at, :], gbt[second, :]], axis=0)
            low = jnp.concatenate([gbt[third, :], gbt[fourth, :]], axis=0)
            out = dot(t_rb[0], high) + dot(t_rb[0], low) + dot(t_rb[1], high)
            send_b[c, s] = out.astype(BF16).reshape(grid, 16, feats)
        exchange(3, c, send_b, recv_b)
        for j in range(groups):
            dz, dm = dz_of(j), dm_of(j)
            dw2[j] += dot_tn(act1[c, :, wide(j)], dz)
            dw1[j] += dot_tn(both_parts(spec.at[c], j), dm)

    def near_of(s, off, size):
        return w_in.at[pl.ds(pl.multiple_of(off, 16), size), pl.ds(s * FT, FT)]

    def near_mixing(off, size):
        return ds_near.at[pl.ds(pl.multiple_of(off, 16), size)]

    segments = [
        Reducer(
            dm_acc.at[s], (act_s.at[:, pl.ds(s * FT, FT)], gh_s.at[:, pl.ds(s * FT, FT)]), dm_land.at[s], functools.partial(near_of, s),
            dm_send.at[s], dm_recv.at[s], order if s < blocks // 2 else swapped, index,
        )
        for s in range(blocks)
    ]

    def all_of(group, k):
        for one in group:
            one.ticks()[k]()

    mix_piece, vec_piece = mix_rows // (2 * grid), 16 * groups // (2 * grid)
    half_side = lax.rem(index["batch"], 2)

    def partner(bit):
        side = lax.rem(index["batch"] // 2**bit, 2)
        return {"batch": index["batch"] + (1 - 2 * side) * 2**bit}

    def late_copy(step, source, target, device):
        return pltpu.make_async_remote_copy(
            src_ref=source, dst_ref=target, send_sem=late_send.at[step], recv_sem=late_recv.at[step],
            device_id=device, device_id_type=MESH,
        )

    def late_halves(bit):
        return late_copy(bit, late_stage.at[bit], late_land.at[bit], partner(bit))

    def late_pieces(step, k):
        peer = lax.rem(me + k, grid)
        if step == batch_bits:
            return late_copy(step, late_split.at[peer], late_parts.at[me], {"grid": peer})
        return late_copy(step, late_near.at[me], late_near.at[me], {"grid": peer})

    def late_home():
        return late_copy(batch_bits + 2, late_near, late_far, partner(0))

    def late_first():
        late_acc[...] = jnp.zeros_like(late_acc)
        for layer, big in enumerate((dw1, dw2)):
            for j in range(groups):
                real = big[j, :128, :128] + big[j, 128:, 128:]
                imag = big[j, :128, 128:] - big[j, 128:, :128]
                for r, part in enumerate((real, imag)):
                    part = jnp.where(pick_lane < BSIZE, part[:BSIZE], part[BSIZE:])
                    for o in range(0, BSIZE, mix_piece):
                        row = ((layer * 2 + r) * groups + j) * BSIZE + o
                        n = min(mix_piece, BSIZE)
                        piece, into = row // mix_piece, row % mix_piece
                        late_acc[piece // grid, piece % grid, into : into + n, :] = part[o : o + n]
        for row in range(SB1, 16):
            dvec[row : row + 1, :] = jnp.sum(sums[row], axis=0, keepdims=True)
        vectors = jnp.concatenate([dvec[:, lanes(j)] for j in range(groups)], axis=0)
        for piece in range(2 * grid):
            late_acc[piece // grid, piece % grid, mix_piece : mix_piece + vec_piece, :] = vectors[
                piece * vec_piece : (piece + 1) * vec_piece
            ]
        late_stage[0] = late_acc[1 - half_side].astype(BF16)
        late_halves(0).start()

    def late_second():
        late_halves(0).wait_recv()
        total = late_acc[half_side] + late_land[0].astype(F32)
        for bit in range(1, batch_bits):
            late_stage[bit] = total.astype(BF16)
            late_halves(bit).start()
            late_halves(bit).wait_recv()
            total = late_stage[bit].astype(F32) + late_land[bit].astype(F32)
        late_split[...] = total.astype(BF16)

        @pl.loop(1, grid)
        def _(k):
            late_pieces(batch_bits, k).start()

    def late_wait(ref, step):
        part = ref.at[pl.ds(0, grid - 1)]
        pltpu.make_async_copy(part, part, late_recv.at[step]).wait()

    def late_third():
        late_wait(late_parts, batch_bits)
        late_parts[me] = late_split[me]
        total = late_parts[0].astype(F32)
        for g in range(1, grid):
            total = total + late_parts[g].astype(F32)
        late_near[me] = total.astype(BF16)

        @pl.loop(1, grid)
        def _(k):
            late_pieces(batch_bits + 1, k).start()

    def late_fourth():
        late_wait(late_near, batch_bits + 1)
        late_home().start()

    def late_fifth():
        late_home().wait_recv()

    def late_sent():
        for bit in range(batch_bits):
            late_halves(bit).wait_send()

        @pl.loop(1, grid)
        def _(k):
            late_pieces(batch_bits, k).wait_send()
            late_pieces(batch_bits + 1, k).wait_send()

        late_home().wait_send()

    queues = {
        "e": [functools.partial(all_of, segments[0::2], k) for k in range(len(segments[0].ticks()))],
        "f": [functools.partial(all_of, segments[1::2], k) for k in range(len(segments[0].ticks()))],
        "l": [late_first, late_second, late_third, late_fourth, late_fifth],
    }

    def run(names):
        for name in names:
            if queues[name]:
                queues[name].pop(0)()

    def finish_inputs(c):
        arrived(3, c, recv_b)
        for s in range(subs):
            cells = pl.ds(s * sz.sub_cells, sz.sub_cells)
            got = recv_b[c, s].reshape(grid * 16, feats)
            hid_s[cells, :] = dot(t_b[0], got) + dot(t_b[1], got)

        @each_tile(CELLS)
        def _(t):
            at = row_tile(t)
            xhat, scale = moments(x_v[c, at, :].astype(F32))
            grad = hid_s[at, :]
            sums[GAIN1] += eight_rows(grad * xhat)
            sums[BIAS1] += eight_rows(grad)
            gres[c, at, :] += pull_norm(grad, xhat, scale, gain1[...])

        pltpu.make_async_copy(gres.at[c], ig_hbm.at[c], sem_ig.at[c]).start()

    @pl.loop(0, 2 * chunks)
    def _(c):
        @pl.when(c < chunks)
        def _():
            feed_forward(c)

        @pl.when(c == chunks - 1)
        def _():
            run("ef")

        @pl.when(jnp.logical_and(c >= 2, c < chunks + 2))
        def _():
            mix_backward(c - 2)

        @pl.when(c == chunks - 1)
        def _():
            run("e")

        @pl.when(c == chunks)
        def _():
            run("fe")

        @pl.when(c == chunks + 1)
        def _():
            run("l")

        @pl.when(c >= chunks)
        def _():
            finish_inputs(c - chunks)

        for k, names in enumerate(("fe", "felfe", "felfelfel")[: chunks - 1]):

            @pl.when(c == chunks + k)
            def _():
                run(names)

    last = [jnp.sum(sums[row], axis=0, keepdims=True) for row in (GAIN1, BIAS1)]
    own = jnp.concatenate([last[k % 2][:, 128 * (k // 2) : 128 * (k // 2) + 128] for k in range(2 * groups)], axis=0)
    n1_send[...] = own
    n1_recv[my_place] = own

    def n1_copy(k):
        return pltpu.make_async_remote_copy(
            src_ref=n1_send, dst_ref=n1_recv.at[my_place], send_sem=n1_ssem, recv_sem=n1_rsem,
            device_id=other(k), device_id_type=MESH,
        )

    @pl.loop(1, everyone)
    def _(k):
        n1_copy(k).start()

    while any(queues.values()):
        run("lef")
    for side, held in enumerate((late_near, late_far)):
        place = half_side if side == 0 else 1 - half_side
        dspec_out[place] = held[:, :mix_piece, :].reshape(mix_rows // 2, 128)
        for g in range(grid):
            late_acc[place, g, mix_piece : mix_piece + vec_piece, :] = held[
                g, mix_piece : mix_piece + vec_piece, :
            ].astype(F32)
    for piece in range(2 * grid):
        for k in range(vec_piece):
            row = piece * vec_piece + k
            dvec_out[row % 16, lanes(row // 16)] = late_acc[piece // grid, piece % grid, mix_piece + k, :]
    part = n1_recv.at[pl.ds(0, everyone - 1)]
    pltpu.make_async_copy(part, part, n1_rsem).wait()
    total = n1_recv[0]
    for g in range(1, everyone):
        total = total + n1_recv[g]
    for j in range(groups):
        dvec_out[0:2, lanes(j)] = total[2 * j : 2 * j + 2, :]

    outs = []
    halves_of = blocks // 2
    for half, turned in zip(range(halves_of), (n2, n2t)):
        near_in, near_out = [pl.ds((half + m * halves_of) * FT, FT) for m in range(2)]
        outs.append(pltpu.make_async_copy(w_in.at[:, near_in], near_hbm.at[half], sem_dm.at[half]))
        outs[-1].start()
        turned[...] = w_in[:, near_out].T
        outs.append(pltpu.make_async_copy(turned, near_hbm.at[halves_of + half], sem_dm.at[halves_of + half]))
        outs[-1].start()

    for one in segments:
        one.wait_sent()
    late_sent()

    @pl.loop(1, everyone)
    def _(k):
        n1_copy(k).wait_send()

    @pl.loop(0, chunks)
    def _(c):
        sent(2, c, send_a)
        sent(3, c, send_b)
        pltpu.make_async_copy(cot_v.at[c], act_hbm.at[c], sem_out.at[c]).wait()
        pltpu.make_async_copy(gres.at[c], ig_hbm.at[c], sem_ig.at[c]).wait()

    for copy in outs:
        copy.wait()


def finish(
    sz,
    act_in, ig_in, near_in, dspec, dvec,
    act_hbm, ig_hbm, gain1, bias1, sw1, sb1, sw2, sb2, gain2, bias2, dmi_hbm, b_in, dmo_hbm, b_out,
    act_v, ig_v, near_v, near_f, sem_in, sem_out,
):
    chunks, feats, hidden = sz.chunks, sz.feats, sz.hidden
    widened = widen(near_in, near_v, near_f, dmi_hbm, dmo_hbm, lax.rem(lax.axis_index("batch"), 2), sem_in, sem_out)
    moves = []
    for c in range(chunks):
        for m, (source, held, target) in enumerate(((ig_in, ig_v, ig_hbm), (act_in, act_v, act_hbm))):
            k = 2 * near_v.shape[0] + 2 * c + m
            moves.append(
                (
                    pltpu.make_async_copy(source.at[c], held.at[c], sem_in.at[k]),
                    pltpu.make_async_copy(held.at[c], target.at[c], sem_out.at[k]),
                )
            )
    next(widened)
    for fetch, store in moves:
        fetch.start()
    for layer, out in enumerate((sw1, sw2)):
        for side in range(2):
            row = lax.broadcasted_iota(jnp.int32, (128, BSIZE), 0)
            lane = lax.broadcasted_iota(jnp.int32, (128, BSIZE), 1)
            pick = (row == lane + BSIZE * side).astype(F32).astype(BF16)
            picked = dot(dspec[layer], pick)
            for r in range(2):
                for j in range(BLOCKS // 2):
                    at = (r * (BLOCKS // 2) + j) * BSIZE
                    out[r, 2 * j + side] = picked[at : at + BSIZE]
    for row, out in ((GAIN1, gain1), (BIAS1, bias1), (GAIN2, gain2), (BIAS2, bias2), (BOUT, b_out)):
        out[...] = dvec[row : row + 1, :]
    sb1[...] = dvec[SB1 : SB1 + 2, :]
    sb2[...] = dvec[SB2 : SB2 + 2, :]
    for f in range(hidden // feats):
        b_in[:, f * feats : (f + 1) * feats] = dvec[BIN + f : BIN + f + 1, :]
    next(widened)
    for fetch, store in moves:
        fetch.wait()
        store.start()
    for fetch, store in moves:
        store.wait()
    for _ in widened:
        pass


def widen(source, held, wide, dmi_hbm, dmo_hbm, side, sem_in, sem_out):
    halves_of, feats = source.shape[0] // 2, source.shape[1]
    rows = feats // 2
    moves = []
    for block in range(2 * halves_of):
        at = pl.ds(pl.multiple_of((2 * (block % halves_of) + side) * FT, FT), FT)
        for part in range(2):
            here = pl.ds(part * rows, rows)
            if block < halves_of:
                target = dmi_hbm.at[here, at]
            else:
                target = dmo_hbm.at[pl.ds(pl.multiple_of((2 * (block % halves_of) + side) * FT + part * rows, rows), rows)]
            k = 2 * block + part
            moves.append(
                (
                    pltpu.make_async_copy(source.at[block, here], held.at[block, here], sem_in.at[k]),
                    pltpu.make_async_copy(wide.at[block, here], target, sem_out.at[k]), block, here,
                )
            )
    for fetch, store, block, here in moves:
        fetch.start()
    yield
    for fetch, store, block, here in moves:
        fetch.wait()
        for o in range(0, rows, COPY):
            at = pl.ds(here.start + o, COPY)
            wide[block, at, :] = held[block, at, :].astype(F32)
        store.start()
    yield
    for fetch, store, block, here in moves:
        store.wait()


def finish_far(far_in, dmi_in, dmo_in, dmi_hbm, dmo_hbm, far_v, far_f, sem_in, sem_out):
    side = 1 - lax.rem(lax.axis_index("batch"), 2)
    for _ in widen(far_in, far_v, far_f, dmi_hbm, dmo_hbm, side, sem_in, sem_out):
        pass


def local(
    batch, grid,
    inputs, cotangent, dataset_ids, channel_masks, sample_counts, norm1_gain, norm1_bias,
    spec_w1, spec_b1, spec_w2, spec_b2, norm2_gain, norm2_bias, mlp_in, mlp_in_bias, mlp_out, mlp_out_bias,
):
    items, rows, cols, feats = inputs.shape
    hidden = mlp_in.shape[1]
    sz = sizes_of(items, rows, cols, feats, hidden, grid)
    batch_bits, grid_bits = batch.bit_length() - 1, grid.bit_length() - 1
    bits = batch_bits + grid_bits

    vmem = pl.BlockSpec(memory_space=pltpu.VMEM)
    smem = pl.BlockSpec(memory_space=pltpu.SMEM)
    hbm = pl.BlockSpec(memory_space=pl.ANY)
    chunks, groups, blocks = sz.chunks, feats // 128, hidden // FT
    shape = (chunks, CELLS, feats)
    pieces = (chunks, sz.subs, grid, 16, feats)
    seg_rows = 2 * feats
    mix_rows = 4 * groups * BSIZE
    late = (grid, mix_rows // (2 * grid) + 16, 128)
    out_shape = (
        jax.ShapeDtypeStruct(shape, BF16),
        jax.ShapeDtypeStruct(shape, F32),
        jax.ShapeDtypeStruct((blocks, feats, FT), BF16),
        jax.ShapeDtypeStruct((2, mix_rows // 2, 128), BF16),
        jax.ShapeDtypeStruct((16, feats), F32),
    )
    dma = pltpu.SemaphoreType.DMA
    scratch = [
        pltpu.VMEM(shape, BF16),
        pltpu.VMEM(shape, BF16),
        pltpu.VMEM(mlp_in.shape, BF16),
        pltpu.VMEM(mlp_out.shape, BF16),
        *[pltpu.VMEM(pieces, BF16)] * 4,
        pltpu.VMEM(shape, F32),
        pltpu.VMEM((chunks, 2, sz.modes, feats), BF16),
        pltpu.VMEM((chunks, sz.modes, 2 * feats), BF16),
        pltpu.VMEM((chunks, sz.modes, 2 * feats), F32),
        pltpu.VMEM((chunks, sz.modes, 2 * feats), F32),
        pltpu.VMEM((groups, 256, 256), BF16),
        pltpu.VMEM((groups, 256, 256), BF16),
        pltpu.VMEM((groups, 256, 256), F32),
        pltpu.VMEM((groups, 256, 256), F32),
        pltpu.VMEM((CELLS, feats), BF16),
        pltpu.VMEM((feats, CELLS), BF16),
        pltpu.VMEM((CELLS, feats), BF16),
        pltpu.VMEM((feats, CELLS), BF16),
        pltpu.VMEM((CELLS, hidden), BF16),
        pltpu.VMEM((CELLS, hidden), BF16),
        pltpu.VMEM((items, 1, feats), F32),
        pltpu.VMEM((items, 1, feats), F32),
        pltpu.VMEM((blocks, seg_rows, FT), F32),
        pltpu.VMEM((blocks, landing_rows(seg_rows, bits), FT), BF16),
        pltpu.VMEM((2, *late), F32),
        pltpu.VMEM((batch_bits, *late), BF16),
        pltpu.VMEM((batch_bits, *late), BF16),
        *[pltpu.VMEM(late, BF16)] * 4,
        pltpu.VMEM((16, feats), F32),
        pltpu.VMEM((16, 8, feats), F32),
        pltpu.VMEM((CELLS, FT), F32),
        pltpu.VMEM((CELLS, FT), F32),
        pltpu.VMEM((2 * groups, 128), F32),
        pltpu.VMEM((batch * grid, 2 * groups, 128), F32),
        dma((chunks,)),
        dma((chunks,)),
        dma((2,)),
        dma((chunks,)),
        dma((chunks,)),
        dma((blocks,)),
        *[dma((4, chunks))] * 2,
        dma((blocks, 2 * bits)),
        dma((blocks, 2 * bits)),
        dma((batch_bits + 3,)),
        dma((batch_bits + 3,)),
        dma,
        dma,
    ]
    cells = items * rows * cols
    row = lambda v: v.reshape(1, -1)
    parts = pl.pallas_call(
        functools.partial(kernel, sz, batch_bits, grid_bits),
        out_shape=out_shape,
        in_specs=[smem] * 3 + [hbm, hbm] + [vmem] * 14 + [hbm, hbm],
        out_specs=(hbm, hbm, hbm, vmem, vmem),
        scratch_shapes=scratch,
        cost_estimate=pl.CostEstimate(
            flops=14 * cells * feats * hidden, bytes_accessed=24 << 20, transcendentals=3 * cells * hidden
        ),
        compiler_params=pltpu.CompilerParams(
            collective_id=0, has_side_effects=True, vmem_limit_bytes=67_000_000
        ),
    )(
        dataset_ids, channel_masks.T, sample_counts,
        inputs.reshape(shape), cotangent.reshape(shape),
        row(norm1_gain), row(norm1_bias), row(norm2_gain), row(norm2_bias),
        spec_w1, spec_b1, spec_w2, spec_b2, row(mlp_in_bias), row(mlp_out_bias),
        *[jnp.asarray(t) for t in tables(sz)], mlp_in, mlp_out,
    )
    vector = jax.ShapeDtypeStruct((1, feats), F32)
    pair = jax.ShapeDtypeStruct((2, feats), F32)
    mixers = jax.ShapeDtypeStruct(spec_w1.shape, F32)
    moves = 2 * blocks + 2 * chunks
    half_shape = (blocks, feats, FT)
    outs = pl.pallas_call(
        functools.partial(finish, sz),
        out_shape=(
            out_shape[0], out_shape[1], vector, vector, mixers, pair, mixers, pair, vector, vector,
            jax.ShapeDtypeStruct(mlp_in.shape, F32), jax.ShapeDtypeStruct((1, hidden), F32),
            jax.ShapeDtypeStruct(mlp_out.shape, F32), vector,
        ),
        in_specs=[hbm] * 3 + [vmem] * 2,
        out_specs=(hbm, hbm) + (vmem,) * 8 + (hbm, vmem, hbm, vmem),
        scratch_shapes=[
            pltpu.VMEM(shape, BF16), pltpu.VMEM(shape, F32), pltpu.VMEM(half_shape, BF16), pltpu.VMEM(half_shape, F32),
            dma((moves,)), dma((moves,)),
        ],
        cost_estimate=pl.CostEstimate(flops=0, bytes_accessed=24 << 20, transcendentals=0),
        compiler_params=pltpu.CompilerParams(vmem_limit_bytes=67_000_000),
    )(*parts)
    far = lax.ppermute(parts[2], "batch", [(b, b ^ 1) for b in range(batch)])
    wide = (jax.ShapeDtypeStruct(mlp_in.shape, F32), jax.ShapeDtypeStruct(mlp_out.shape, F32))
    dmi, dmo = pl.pallas_call(
        finish_far,
        out_shape=wide,
        in_specs=[hbm] * 3,
        out_specs=(hbm, hbm),
        input_output_aliases={1: 0, 2: 1},
        scratch_shapes=[
            pltpu.VMEM(half_shape, BF16), pltpu.VMEM(half_shape, F32), dma((2 * blocks,)), dma((2 * blocks,)),
        ],
        cost_estimate=pl.CostEstimate(flops=0, bytes_accessed=6 << 20, transcendentals=0),
        compiler_params=pltpu.CompilerParams(vmem_limit_bytes=67_000_000),
    )(far, outs[10], outs[12])
    flat = lambda v: v.reshape(-1)
    return (
        outs[0].reshape(inputs.shape), outs[1].reshape(inputs.shape), flat(outs[2]), flat(outs[3]), *outs[4:8],
        flat(outs[8]), flat(outs[9]), dmi, flat(outs[11]), dmo, flat(outs[13]),
    )


def solution(mesh):
    spread = P("batch", "grid", None, None)
    return jax.shard_map(
        functools.partial(local, mesh.shape["batch"], mesh.shape["grid"]),
        mesh=mesh,
        in_specs=(spread, spread, P("batch")) + (P(),) * 14,
        out_specs=(spread, spread) + (P(),) * 12,
        check_vma=False,
    )
```

time: 671 us -> 247 us (0.37)
  waiting for transfers between devices: 247 us -> 0.01 us
  Pallas kernels: 0 us -> 246 us
  matrix products: 153 us -> 0 us
  local copies, waits for them, and re-layouts: 122 us -> 0 us
  blocking collectives: 52.8 us -> 0 us
  starting transfers between devices: 39.2 us -> 0.07 us
  other arithmetic: 35.2 us -> 0 us
  between operations: 15.2 us -> 0.84 us
    pallas_call x0 -> x3, Pallas kernels: none -> 246 us  [the longest x1 234 us: local(): pl.pallas_call(functools.partial(kernel, sz, batch_bits, grid_bits), out_...]
    dot_general x22 -> x0, matrix products: 153 us -> none  [the longest x1 41.5 us: local(): jnp.dot(normed_two_bf, mlp_in, preferred_element_type=jnp.float32)]
    all_to_all x4 -> x0, waiting for transfers between devices: 148 us -> none  [the longest x1 40.3 us: local(): lax.all_to_all(col_spec, 'grid', split_axis=2, concat_axis=1, tiled=True)]
    psum x1 -> x0, waiting for transfers between devices: 98.5 us -> none  [local(): summed = tuple(lax.psum(mixer_grads + mlp_grads, ('batch', 'grid')))]
    psum x1 -> x0, blocking collectives: 52.8 us -> none  [local(): summed = tuple(lax.psum(mixer_grads + mlp_grads, ('batch', 'grid')))]
    convert_element_type x10 -> x0, local copies, waits for them, and re-layouts: 40.7 us -> none  [the longest x2 10.5 us: local(): row_back.reshape(count_here, height, mode_cols, 2 * feat_dim)]
    all_to_all x4 -> x0, starting transfers between devices: 39 us -> none  [the longest x1 10.5 us: local(): lax.all_to_all(row_back, 'grid', split_axis=1, concat_axis=2, tiled=True)]
    reshape x11 -> x0, local copies, waits for them, and re-layouts: 38.7 us -> none  [the longest x2 9.28 us: local(): grad_shrunk.reshape(mixed_two.shape)]
  transfers between devices with their start and end apart: 5 -> 1, of which waited for: 5 -> 0; matrix products, arithmetic and copies ran while one was open for 8% -> 0% of each run, Pallas kernels for 0% -> 4%
where the time goes in v1:
time: 247 us
  Pallas kernels  246 us (100%)
    pallas_call x1, Pallas kernels, local(): pl.pallas_call(functools.partial(kernel, sz, batch_bits, grid_bits), out_...  234 us
    pallas_call x1, Pallas kernels, local(): pl.pallas_call(functools.partial(finish, sz), out_shape=(out_shape[0], ou...  9.22 us
  transfers between devices with their start and end apart: 1, of which 0 were waited for; matrix products, arithmetic and copies ran while one was open for 0% of the time, Pallas kernels for 4%

profile of v1, /device:TPU:0, one launch (start us, length us, event | category | flops | bytes accessed | tf_op | source)
XLA Modules:
  0.0 246.9 jit_solution(3449270304909637402)
XLA Ops:
  0.7 233.6 %shard_map.308 = (bf16[4,512,512]{2,1,0:T(8,128)(2,1)}, f32[4,512,512]{2,1,0:T(8,128)}, bf16[4,512,512]{2,1,0:T(8,128)(2,1)}, bf16[2,512,128]{2,1,0:T(8,128)(2,1)}, f32[16,512]{1,0:T(8,128)}) custom-call(s32[8]{0:T(128)} %ids.1, s32[4,12]{1,0:T(4,128)} %bitcast.23, s32[12]{0:T(128)} %counts.1, bf16[4,512,512]{2,1,0:T(8,128)(2,1)} %bitcast.18, ...), custom_call_target="tpu_custom_call" | custom-call | flops 30064771072 | bytes 25165824 | tf_op jit(solution)/shard_map/pallas_call | solution.py:1023
  234.3 0.1 collective-permute-start
  234.4 9.2 %shard_map.309 = (bf16[4,512,512]{2,1,0:T(8,128)(2,1)}, f32[4,512,512]{2,1,0:T(8,128)}, f32[1,512]{1,0:T(1,128)}, f32[1,512]{1,0:T(1,128)}, f32[2,8,64,64]{3,2,1...) custom-call(bf16[4,512,512]{2,1,0:T(8,128)(2,1)} %get-tuple-element., ...), custom_call_target="tpu_custom_call" | custom-call | bytes 25165824 | tf_op jit(solution)/shard_map/pallas_call | solution.py:1047
  243.6 0.0 collective-permute-done.far_in
  243.6 3.1 %shard_map.310 = (f32[512,2048]{1,0:T(8,128)}, f32[2048,512]{1,0:T(8,128)}) custom-call(bf16[4,512,512]{2,1,0:T(8,128)(2,1)} %collective-permute-done.far_in, f32[512,2048]{1,0:T(8,128)} %get-tuple-element.50.dmi_in, f32[2048,512]{1,0:T(8,128)} %get-tuple-element.51.dmo_in), custom_call_target="tpu_custom_call", output_to_operand_aliasing={{0}: (1, {}), {1}: (2, {})} | custom-call | bytes 6291456 | tf_op jit(solution)/shard_map/pallas_call | solution.py:1065
Async XLA Ops:
  234.3 9.3 %collective-permute-start = (bf16[4,512,512]{2,1,0:T(8,128)(2,1)}, bf16[4,512,512]{2,1,0:T(8,128)(2,1)}, u32[]{:S(2)}, u32[]{:S(2)}) collective-permute-start(bf16[4,512,512]{2,1,0:T(8,128)(2,1)} %get-tuple-element.37.near_in), channel_id=1, source_target_pairs={{0,16},{16,0},{1,17},{17,1},{2,18},{18,2},{3,19},{19,3},{4,20},{20... | collective-permute-start | bytes 6291464 | tf_op jit(solution)/shard_map/ppermute | solution.py:1063

commit v2 on v1

--- a/solution.py
+++ b/solution.py
@@ -27,6 +27,8 @@
     sz = type("Sizes", (), {})()
     sz.items, sz.rows, sz.cols, sz.feats, sz.hidden, sz.grid = items, rows, cols, feats, hidden, grid
     sz.own = MODES // grid
+    sz.plane = math.gcd(grid, 4)
+    sz.planes = grid // sz.plane
     sz.height = rows * grid
     sz.item_cells = rows * cols
     sz.sub_items = 16 // (rows * sz.own * 2)
@@ -285,7 +287,7 @@
     x_v, cot_v, w_in, w_out, send_a, recv_a, send_b, recv_b, gres,
     spec, act1, slope1, slope2, w1, w2, dw1, dw2,
     n2, n2t, gb, gbt, act_s, gh_s, live, weight,
-    dm_acc, dm_land, late_acc, late_stage, late_land, late_split, late_parts, late_near, late_far, dvec, sums, hid_s, pul_s, n1_send, n1_recv,
+    dm_acc, dm_land, late_acc, late_stage, late_land, late_split, late_parts, late_sum, late_rows, late_near, late_far, dvec, sums, hid_s, pul_s, n1_send, n1_recv, n1_rows,
     sem_x, sem_cot, sem_w, sem_out, sem_ig, sem_dm, send_sems, recv_sems,
     dm_send, dm_recv, late_send, late_recv, n1_ssem, n1_rsem,
 ):
@@ -321,7 +323,6 @@
         return {"batch": b, "grid": g}
 
     everyone = 2**batch_bits * grid
-    my_place = index["batch"] * grid + me
 
     @pl.loop(1, everyone)
     def _(k):
@@ -333,23 +334,22 @@
             k = grid // 2 + ((j + 1) // 2) * (2 * lax.rem(j + 1, 2) - 1)
             peer = lax.rem(me + k, grid)
             pltpu.make_async_remote_copy(
-                src_ref=send.at[c, :, peer],
-                dst_ref=recv.at[c, :, me],
+                src_ref=send.at[c, peer],
+                dst_ref=recv.at[c, me],
                 send_sem=send_sems.at[stage, c],
                 recv_sem=recv_sems.at[stage, c],
                 device_id={"grid": peer},
                 device_id_type=MESH,
             ).start()
 
-        for s in range(subs):
-            recv[c, s, me] = send[c, s, me]
+        recv[c, me] = send[c, me]
 
     def arrived(stage, c, recv):
-        part = recv.at[c, :, pl.ds(0, grid - 1)]
+        part = recv.at[c, pl.ds(0, grid - 1)]
         pltpu.make_async_copy(part, part, recv_sems.at[stage, c]).wait()
 
     def sent(stage, c, send):
-        part = send.at[c, :, pl.ds(0, grid - 1)]
+        part = send.at[c, pl.ds(0, grid - 1)]
         pltpu.make_async_copy(part, part, send_sems.at[stage, c]).wait()
 
     def doubled(rows, inner):
@@ -373,7 +373,7 @@
             cells = pl.ds(s * sz.sub_cells, sz.sub_cells)
             high = hi_v[cells, :]
             out = dot(table[0], high) + dot(table[0], lo_v[cells, :]) + dot(table[1], high)
-            send[c, s] = out.astype(BF16).reshape(grid, 16, feats)
+            send[c, :, s] = out.astype(BF16).reshape(grid, 16, feats)
 
     def both_parts(ref, j):
         return jnp.concatenate([ref[0, :, lanes(j)], ref[1, :, lanes(j)]], axis=1)
@@ -436,7 +436,7 @@
     def _(c):
         arrived(0, c, recv_a)
         for s in range(subs):
-            got = recv_a[c, s].reshape(grid * 16, feats)
+            got = recv_a[c, :, s].reshape(grid * 16, feats)
             out = (dot(t_rf[0], got) + dot(t_rf[1], got)).astype(BF16)
             at = pl.ds(s * sz.sub_modes, sz.sub_modes)
             spec[c, 0, at, :] = out[: sz.sub_modes]
@@ -471,7 +471,7 @@
             second, third, fourth = [pl.ds(k * modes + s * sz.sub_modes, sz.sub_modes) for k in (1, 2, 3)]
             high = jnp.concatenate([gbt[at, :], gbt[second, :]], axis=0)
             out = (dot(t_rb[0], high) + dot(t_rb[1], high)) * doubled(grid * 16, 2)
-            send_b[c, s] = out.astype(BF16).reshape(grid, 16, feats)
+            send_b[c, :, s] = out.astype(BF16).reshape(grid, 16, feats)
         exchange(1, c, send_b, recv_b)
 
     load_win.wait()
@@ -482,7 +482,7 @@
         arrived(1, c, recv_b)
         for s in range(subs):
             cells = pl.ds(s * sz.sub_cells, sz.sub_cells)
-            got = recv_b[c, s].reshape(grid * 16, feats)
+            got = recv_b[c, :, s].reshape(grid * 16, feats)
             gres[c, cells, :] = dot(t_b[0], got) + dot(t_b[1], got)
 
         @each_tile(CELLS)
@@ -554,7 +554,7 @@
     def mix_backward(c):
         arrived(2, c, recv_a)
         for s in range(subs):
-            got = recv_a[c, s].reshape(grid * 16, feats)
+            got = recv_a[c, :, s].reshape(grid * 16, feats)
             out = (dot(t_rf[0], got) + dot(t_rf[1], got)) * doubled(2 * sz.sub_modes, MODES)
             at = pl.ds(s * sz.sub_modes, sz.sub_modes)
             hid_s[at, :] = out[: sz.sub_modes]
@@ -604,7 +604,7 @@
             high = jnp.concatenate([gbt[at, :], gbt[second, :]], axis=0)
             low = jnp.concatenate([gbt[third, :], gbt[fourth, :]], axis=0)
             out = dot(t_rb[0], high) + dot(t_rb[0], low) + dot(t_rb[1], high)
-            send_b[c, s] = out.astype(BF16).reshape(grid, 16, feats)
+            send_b[c, :, s] = out.astype(BF16).reshape(grid, 16, feats)
         exchange(3, c, send_b, recv_b)
         for j in range(groups):
             dz, dm = dz_of(j), dm_of(j)
@@ -631,6 +631,8 @@
 
     mix_piece, vec_piece = mix_rows // (2 * grid), 16 * groups // (2 * grid)
     half_side = lax.rem(index["batch"], 2)
+    plane, planes = sz.plane, sz.planes
+    my_z, my_p = me // plane, lax.rem(me, plane)
 
     def partner(bit):
         side = lax.rem(index["batch"] // 2**bit, 2)
@@ -645,14 +647,22 @@
     def late_halves(bit):
         return late_copy(bit, late_stage.at[bit], late_land.at[bit], partner(bit))
 
-    def late_pieces(step, k):
-        peer = lax.rem(me + k, grid)
+    def late_plane(step, k):
+        p = lax.rem(my_p + k, plane)
+        device = {"grid": my_z * plane + p}
         if step == batch_bits:
-            return late_copy(step, late_split.at[peer], late_parts.at[me], {"grid": peer})
-        return late_copy(step, late_near.at[me], late_near.at[me], {"grid": peer})
+            return late_copy(step, late_split.at[:, p], late_parts.at[my_p], device)
+        return late_copy(step, late_near.at[:, my_p], late_near.at[:, my_p], device)
+
+    def late_z(step, k):
+        z = lax.rem(my_z + k, planes)
+        device = {"grid": z * plane + my_p}
+        if step == batch_bits + 1:
+            return late_copy(step, late_sum.at[z], late_rows.at[my_z], device)
+        return late_copy(step, late_near.at[my_z, my_p], late_near.at[my_z, my_p], device)
 
     def late_home():
-        return late_copy(batch_bits + 2, late_near, late_far, partner(0))
+        return late_copy(batch_bits + 4, late_near, late_far, partner(0))
 
     def late_first():
         late_acc[...] = jnp.zeros_like(late_acc)
@@ -685,50 +695,73 @@
             late_halves(bit).start()
             late_halves(bit).wait_recv()
             total = late_stage[bit].astype(F32) + late_land[bit].astype(F32)
-        late_split[...] = total.astype(BF16)
-
-        @pl.loop(1, grid)
+        late_split[...] = total.astype(BF16).reshape(late_split.shape)
+
+        @pl.loop(1, plane)
         def _(k):
-            late_pieces(batch_bits, k).start()
-
-    def late_wait(ref, step):
-        part = ref.at[pl.ds(0, grid - 1)]
+            late_plane(batch_bits, k).start()
+
+    def late_wait(part, step):
         pltpu.make_async_copy(part, part, late_recv.at[step]).wait()
 
     def late_third():
-        late_wait(late_parts, batch_bits)
-        late_parts[me] = late_split[me]
+        late_wait(late_parts.at[pl.ds(0, plane - 1)], batch_bits)
+        late_parts[my_p] = late_split[:, my_p]
         total = late_parts[0].astype(F32)
-        for g in range(1, grid):
-            total = total + late_parts[g].astype(F32)
-        late_near[me] = total.astype(BF16)
-
-        @pl.loop(1, grid)
+        for k in range(1, plane):
+            total = total + late_parts[k].astype(F32)
+        late_sum[...] = total.astype(BF16)
+
+        @pl.loop(1, planes)
         def _(k):
-            late_pieces(batch_bits + 1, k).start()
+            late_z(batch_bits + 1, k).start()
 
     def late_fourth():
-        late_wait(late_near, batch_bits + 1)
+        late_wait(late_rows.at[pl.ds(0, planes - 1)], batch_bits + 1)
+        late_rows[my_z] = late_sum[my_z]
+        total = late_rows[0].astype(F32)
+        for k in range(1, planes):
+            total = total + late_rows[k].astype(F32)
+        late_near[my_z, my_p] = total.astype(BF16)
+
+        @pl.loop(1, planes)
+        def _(k):
+            late_z(batch_bits + 2, k).start()
+
+    def late_fifth():
+        late_wait(late_near.at[pl.ds(0, planes - 1), my_p], batch_bits + 2)
+
+        @pl.loop(1, plane)
+        def _(k):
+            late_plane(batch_bits + 3, k).start()
+
+    def late_sixth():
+        late_wait(late_near.at[:, pl.ds(0, plane - 1)], batch_bits + 3)
         late_home().start()
 
-    def late_fifth():
+    def late_seventh():
         late_home().wait_recv()
 
     def late_sent():
         for bit in range(batch_bits):
             late_halves(bit).wait_send()
 
-        @pl.loop(1, grid)
+        @pl.loop(1, plane)
         def _(k):
-            late_pieces(batch_bits, k).wait_send()
-            late_pieces(batch_bits + 1, k).wait_send()
+            late_plane(batch_bits, k).wait_send()
+            late_plane(batch_bits + 3, k).wait_send()
+
+        @pl.loop(1, planes)
+        def _(k):
+            late_z(batch_bits + 1, k).wait_send()
+            late_z(batch_bits + 2, k).wait_send()
 
         late_home().wait_send()
 
     queues = {
         "e": [functools.partial(all_of, segments[0::2], k) for k in range(len(segments[0].ticks()))],
         "f": [functools.partial(all_of, segments[1::2], k) for k in range(len(segments[0].ticks()))],
-        "l": [late_first, late_second, late_third, late_fourth, late_fifth],
+        "l": [late_first, late_second, late_third, late_fourth, late_fifth, late_sixth, late_seventh],
     }
 
     def run(names):
@@ -740,7 +773,7 @@
         arrived(3, c, recv_b)
         for s in range(subs):
             cells = pl.ds(s * sz.sub_cells, sz.sub_cells)
-            got = recv_b[c, s].reshape(grid * 16, feats)
+            got = recv_b[c, :, s].reshape(grid * 16, feats)
             hid_s[cells, :] = dot(t_b[0], got) + dot(t_b[1], got)
 
         @each_tile(CELLS)
@@ -792,37 +825,62 @@
 
     last = [jnp.sum(sums[row], axis=0, keepdims=True) for row in (GAIN1, BIAS1)]
     own = jnp.concatenate([last[k % 2][:, 128 * (k // 2) : 128 * (k // 2) + 128] for k in range(2 * groups)], axis=0)
-    n1_send[...] = own
-    n1_recv[my_place] = own
-
-    def n1_copy(k):
+    near_count = 2**batch_bits * plane
+    n1_send[0] = own
+    n1_recv[index["batch"] * plane + my_p] = own
+
+    def n1_near(k):
+        device = {
+            "batch": lax.rem(index["batch"] + k // plane, 2**batch_bits),
+            "grid": my_z * plane + lax.rem(my_p + lax.rem(k, plane), plane),
+        }
         return pltpu.make_async_remote_copy(
-            src_ref=n1_send, dst_ref=n1_recv.at[my_place], send_sem=n1_ssem, recv_sem=n1_rsem,
-            device_id=other(k), device_id_type=MESH,
+            src_ref=n1_send.at[0], dst_ref=n1_recv.at[index["batch"] * plane + my_p], send_sem=n1_ssem.at[0],
+            recv_sem=n1_rsem.at[0], device_id=device, device_id_type=MESH,
         )
 
-    @pl.loop(1, everyone)
+    def n1_far(k):
+        return pltpu.make_async_remote_copy(
+            src_ref=n1_send.at[1], dst_ref=n1_rows.at[my_z], send_sem=n1_ssem.at[1], recv_sem=n1_rsem.at[1],
+            device_id={"grid": lax.rem(my_z + k, planes) * plane + my_p}, device_id_type=MESH,
+        )
+
+    def n1_wait(part, step):
+        pltpu.make_async_copy(part, part, n1_rsem.at[step]).wait()
+
+    @pl.loop(1, near_count)
     def _(k):
-        n1_copy(k).start()
+        n1_near(k).start()
+
+    run("le")
+    n1_wait(n1_recv.at[pl.ds(0, near_count - 1)], 0)
+    total = n1_recv[0]
+    for k in range(1, near_count):
+        total = total + n1_recv[k]
+    n1_send[1] = total
+    n1_rows[my_z] = total
+
+    @pl.loop(1, planes)
+    def _(k):
+        n1_far(k).start()
 
     while any(queues.values()):
         run("lef")
     for side, held in enumerate((late_near, late_far)):
         place = half_side if side == 0 else 1 - half_side
-        dspec_out[place] = held[:, :mix_piece, :].reshape(mix_rows // 2, 128)
+        dspec_out[place] = held[:, :, :mix_piece, :].reshape(mix_rows // 2, 128)
         for g in range(grid):
             late_acc[place, g, mix_piece : mix_piece + vec_piece, :] = held[
-                g, mix_piece : mix_piece + vec_piece, :
+                g // plane, g % plane, mix_piece : mix_piece + vec_piece, :
             ].astype(F32)
     for piece in range(2 * grid):
         for k in range(vec_piece):
             row = piece * vec_piece + k
             dvec_out[row % 16, lanes(row // 16)] = late_acc[piece // grid, piece % grid, mix_piece + k, :]
-    part = n1_recv.at[pl.ds(0, everyone - 1)]
-    pltpu.make_async_copy(part, part, n1_rsem).wait()
-    total = n1_recv[0]
-    for g in range(1, everyone):
-        total = total + n1_recv[g]
+    n1_wait(n1_rows.at[pl.ds(0, planes - 1)], 1)
+    total = n1_rows[0]
+    for k in range(1, planes):
+        total = total + n1_rows[k]
     for j in range(groups):
         dvec_out[0:2, lanes(j)] = total[2 * j : 2 * j + 2, :]
 
@@ -840,9 +898,13 @@
         one.wait_sent()
     late_sent()
 
-    @pl.loop(1, everyone)
+    @pl.loop(1, near_count)
     def _(k):
-        n1_copy(k).wait_send()
+        n1_near(k).wait_send()
+
+    @pl.loop(1, planes)
+    def _(k):
+        n1_far(k).wait_send()
 
     @pl.loop(0, chunks)
     def _(c):
@@ -957,10 +1019,11 @@
     hbm = pl.BlockSpec(memory_space=pl.ANY)
     chunks, groups, blocks = sz.chunks, feats // 128, hidden // FT
     shape = (chunks, CELLS, feats)
-    pieces = (chunks, sz.subs, grid, 16, feats)
+    pieces = (chunks, grid, sz.subs, 16, feats)
     seg_rows = 2 * feats
     mix_rows = 4 * groups * BSIZE
     late = (grid, mix_rows // (2 * grid) + 16, 128)
+    plane, planes = sz.plane, sz.planes
     out_shape = (
         jax.ShapeDtypeStruct(shape, BF16),
         jax.ShapeDtypeStruct(shape, F32),
@@ -997,13 +1060,18 @@
         pltpu.VMEM((2, *late), F32),
         pltpu.VMEM((batch_bits, *late), BF16),
         pltpu.VMEM((batch_bits, *late), BF16),
-        *[pltpu.VMEM(late, BF16)] * 4,
+        pltpu.VMEM((planes, plane, *late[1:]), BF16),
+        pltpu.VMEM((plane, planes, *late[1:]), BF16),
+        pltpu.VMEM((planes, *late[1:]), BF16),
+        pltpu.VMEM((planes, *late[1:]), BF16),
+        *[pltpu.VMEM((planes, plane, *late[1:]), BF16)] * 2,
         pltpu.VMEM((16, feats), F32),
         pltpu.VMEM((16, 8, feats), F32),
         pltpu.VMEM((CELLS, FT), F32),
         pltpu.VMEM((CELLS, FT), F32),
-        pltpu.VMEM((2 * groups, 128), F32),
-        pltpu.VMEM((batch * grid, 2 * groups, 128), F32),
+        pltpu.VMEM((2, 2 * groups, 128), F32),
+        pltpu.VMEM((batch * plane, 2 * groups, 128), F32),
+        pltpu.VMEM((planes, 2 * groups, 128), F32),
         dma((chunks,)),
         dma((chunks,)),
         dma((2,)),
@@ -1013,10 +1081,10 @@
         *[dma((4, chunks))] * 2,
         dma((blocks, 2 * bits)),
         dma((blocks, 2 * bits)),
-        dma((batch_bits + 3,)),
-        dma((batch_bits + 3,)),
-        dma,
-        dma,
+        dma((batch_bits + 5,)),
+        dma((batch_bits + 5,)),
+        dma((2,)),
+        dma((2,)),
     ]
     cells = items * rows * cols
     row = lambda v: v.reshape(1, -1)

time: 247 us -> 244 us (0.988)
  Pallas kernels: 246 us -> 243 us
    pallas_call x1, Pallas kernels: 234 us -> 231 us  [local(): pl.pallas_call(functools.partial(kernel, sz, batch_bits, grid_bits), out_...]
where the time goes in v2:
time: 244 us
  Pallas kernels  243 us (100%)
    pallas_call x1, Pallas kernels, local(): pl.pallas_call(functools.partial(kernel, sz, batch_bits, grid_bits), out_...  231 us
    pallas_call x1, Pallas kernels, local(): pl.pallas_call(functools.partial(finish, sz), out_shape=(out_shape[0], ou...  9.22 us
  transfers between devices with their start and end apart: 1, of which 0 were waited for; matrix products, arithmetic and copies ran while one was open for 0% of the time, Pallas kernels for 4%

profile of v2, /device:TPU:0, one launch (start us, length us, event | category | flops | bytes accessed | tf_op | source)
XLA Modules:
  0.0 244.2 jit_solution(8973784458396796591)
XLA Ops:
  0.7 230.6 %shard_map.308 = (bf16[4,512,512]{2,1,0:T(8,128)(2,1)}, f32[4,512,512]{2,1,0:T(8,128)}, bf16[4,512,512]{2,1,0:T(8,128)(2,1)}, bf16[2,512,128]{2,1,0:T(8,128)(2,1)}, f32[16,512]{1,0:T(8,128)}) custom-call(s32[8]{0:T(128)} %ids.1, s32[4,12]{1,0:T(4,128)} %bitcast.23, s32[12]{0:T(128)} %counts.1, bf16[4,512,512]{2,1,0:T(8,128)(2,1)} %bitcast.18, ...), custom_call_target="tpu_custom_call" | custom-call | flops 30064771072 | bytes 25165824 | tf_op jit(solution)/shard_map/pallas_call | solution.py:1091
  231.2 0.5 collective-permute-start
  231.7 9.2 %shard_map.309 = (bf16[4,512,512]{2,1,0:T(8,128)(2,1)}, f32[4,512,512]{2,1,0:T(8,128)}, f32[1,512]{1,0:T(1,128)}, f32[1,512]{1,0:T(1,128)}, f32[2,8,64,64]{3,2,1...) custom-call(bf16[4,512,512]{2,1,0:T(8,128)(2,1)} %get-tuple-element., ...), custom_call_target="tpu_custom_call" | custom-call | bytes 25165824 | tf_op jit(solution)/shard_map/pallas_call | solution.py:1115
  240.9 0.0 collective-permute-done.far_in
  241.0 3.1 %shard_map.310 = (f32[512,2048]{1,0:T(8,128)}, f32[2048,512]{1,0:T(8,128)}) custom-call(bf16[4,512,512]{2,1,0:T(8,128)(2,1)} %collective-permute-done.far_in, f32[512,2048]{1,0:T(8,128)} %get-tuple-element.50.dmi_in, f32[2048,512]{1,0:T(8,128)} %get-tuple-element.51.dmo_in), custom_call_target="tpu_custom_call", output_to_operand_aliasing={{0}: (1, {}), {1}: (2, {})} | custom-call | bytes 6291456 | tf_op jit(solution)/shard_map/pallas_call | solution.py:1133
Async XLA Ops:
  231.2 9.7 %collective-permute-start = (bf16[4,512,512]{2,1,0:T(8,128)(2,1)}, bf16[4,512,512]{2,1,0:T(8,128)(2,1)}, u32[]{:S(2)}, u32[]{:S(2)}) collective-permute-start(bf16[4,512,512]{2,1,0:T(8,128)(2,1)} %get-tuple-element.37.near_in), channel_id=1, source_target_pairs={{0,16},{16,0},{1,17},{17,1},{2,18},{18,2},{3,19},{19,3},{4,20},{20... | collective-permute-start | bytes 6291464 | tf_op jit(solution)/shard_map/ppermute | solution.py:1131

commit v3 on v2

--- a/solution.py
+++ b/solution.py
@@ -328,10 +328,11 @@
     def _(k):
         pl.semaphore_signal(barrier, inc=1, device_id=other(k), device_id_type=MESH)
 
+    ranked = sorted(range(1, grid), key=lambda k: abs(k - grid // 2))
+    turns = [ranked[j // 2] if j % 2 == 0 else ranked[-1 - j // 2] for j in range(grid - 1)]
+
     def exchange(stage, c, send, recv):
-        @pl.loop(0, grid - 1)
-        def _(j):
-            k = grid // 2 + ((j + 1) // 2) * (2 * lax.rem(j + 1, 2) - 1)
+        for k in turns:
             peer = lax.rem(me + k, grid)
             pltpu.make_async_remote_copy(
                 src_ref=send.at[c, peer],
@@ -919,11 +920,17 @@
 
 def finish(
     sz,
-    act_in, ig_in, near_in, dspec, dvec,
+    act_in, ig_in, near_in, dspec_in, dvec_in,
     act_hbm, ig_hbm, gain1, bias1, sw1, sb1, sw2, sb2, gain2, bias2, dmi_hbm, b_in, dmo_hbm, b_out,
-    act_v, ig_v, near_v, near_f, sem_in, sem_out,
+    act_v, ig_v, near_v, near_f, dspec, dvec, sem_in, sem_out, sem_small,
 ):
     chunks, feats, hidden = sz.chunks, sz.feats, sz.hidden
+    small = [
+        pltpu.make_async_copy(source, held, sem_small.at[k])
+        for k, (source, held) in enumerate(((dspec_in, dspec), (dvec_in, dvec)))
+    ]
+    for copy in small:
+        copy.start()
     widened = widen(near_in, near_v, near_f, dmi_hbm, dmo_hbm, lax.rem(lax.axis_index("batch"), 2), sem_in, sem_out)
     moves = []
     for c in range(chunks):
@@ -938,6 +945,8 @@
     next(widened)
     for fetch, store in moves:
         fetch.start()
+    for copy in small:
+        copy.wait()
     for layer, out in enumerate((sw1, sw2)):
         for side in range(2):
             row = lax.broadcasted_iota(jnp.int32, (128, BSIZE), 0)
@@ -1119,11 +1128,12 @@
             jax.ShapeDtypeStruct(mlp_in.shape, F32), jax.ShapeDtypeStruct((1, hidden), F32),
             jax.ShapeDtypeStruct(mlp_out.shape, F32), vector,
         ),
-        in_specs=[hbm] * 3 + [vmem] * 2,
+        in_specs=[hbm] * 5,
         out_specs=(hbm, hbm) + (vmem,) * 8 + (hbm, vmem, hbm, vmem),
         scratch_shapes=[
             pltpu.VMEM(shape, BF16), pltpu.VMEM(shape, F32), pltpu.VMEM(half_shape, BF16), pltpu.VMEM(half_shape, F32),
-            dma((moves,)), dma((moves,)),
+            pltpu.VMEM(out_shape[3].shape, BF16), pltpu.VMEM(out_shape[4].shape, F32),
+            dma((moves,)), dma((moves,)), dma((2,)),
         ],
         cost_estimate=pl.CostEstimate(flops=0, bytes_accessed=24 << 20, transcendentals=0),
         compiler_params=pltpu.CompilerParams(vmem_limit_bytes=67_000_000),

time: 244 us -> 244 us (level)
  no operation moved by 1% of the time
where the time goes in v3:
time: 244 us
  Pallas kernels  243 us (100%)
    pallas_call x1, Pallas kernels, local(): pl.pallas_call(functools.partial(kernel, sz, batch_bits, grid_bits), out_...  231 us
    pallas_call x1, Pallas kernels, local(): pl.pallas_call(functools.partial(finish, sz), out_shape=(out_shape[0], ou...  8.68 us
  transfers between devices with their start and end apart: 1, of which 0 were waited for; matrix products, arithmetic and copies ran while one was open for 0% of the time, Pallas kernels for 4%

profile of v3, /device:TPU:0, one launch (start us, length us, event | category | flops | bytes accessed | tf_op | source)
XLA Modules:
  0.0 243.8 jit_solution(5631745340144316142)
XLA Ops:
  0.7 231.0 %shard_map.308 = (bf16[4,512,512]{2,1,0:T(8,128)(2,1)}, f32[4,512,512]{2,1,0:T(8,128)}, bf16[4,512,512]{2,1,0:T(8,128)(2,1)}, bf16[2,512,128]{2,1,0:T(8,128)(2,1)}, f32[16,512]{1,0:T(8,128)}) custom-call(s32[8]{0:T(128)} %ids.1, s32[4,12]{1,0:T(4,128)} %bitcast.23, s32[12]{0:T(128)} %counts.1, bf16[4,512,512]{2,1,0:T(8,128)(2,1)} %bitcast.18, ...), custom_call_target="tpu_custom_call" | custom-call | flops 30064771072 | bytes 25165824 | tf_op jit(solution)/shard_map/pallas_call | solution.py:1100
  231.7 0.2 collective-permute-start
  231.8 8.7 %shard_map.309 = (bf16[4,512,512]{2,1,0:T(8,128)(2,1)}, f32[4,512,512]{2,1,0:T(8,128)}, f32[1,512]{1,0:T(1,128)}, f32[1,512]{1,0:T(1,128)}, f32[2,8,64,64]{3,2,1...) custom-call(bf16[4,512,512]{2,1,0:T(8,128)(2,1)} %get-tuple-element., ...), custom_call_target="tpu_custom_call" | custom-call | bytes 25165824 | tf_op jit(solution)/shard_map/pallas_call | solution.py:1124
  240.5 0.0 collective-permute-done.far_in
  240.5 3.1 %shard_map.310 = (f32[512,2048]{1,0:T(8,128)}, f32[2048,512]{1,0:T(8,128)}) custom-call(bf16[4,512,512]{2,1,0:T(8,128)(2,1)} %collective-permute-done.far_in, f32[512,2048]{1,0:T(8,128)} %get-tuple-element.50.dmi_in, f32[2048,512]{1,0:T(8,128)} %get-tuple-element.51.dmo_in), custom_call_target="tpu_custom_call", output_to_operand_aliasing={{0}: (1, {}), {1}: (2, {})} | custom-call | bytes 6291456 | tf_op jit(solution)/shard_map/pallas_call | solution.py:1143
Async XLA Ops:
  231.7 8.9 %collective-permute-start = (bf16[4,512,512]{2,1,0:T(8,128)(2,1)}, bf16[4,512,512]{2,1,0:T(8,128)(2,1)}, u32[]{:S(2)}, u32[]{:S(2)}) collective-permute-start(bf16[4,512,512]{2,1,0:T(8,128)(2,1)} %get-tuple-element.37.near_in), channel_id=1, source_target_pairs={{0,16},{16,0},{1,17},{17,1},{2,18},{18,2},{3,19},{19,3},{4,20},{20... | collective-permute-start | bytes 6291464 | tf_op jit(solution)/shard_map/ppermute | solution.py:1141
